TPU v7x, 32 devices: a whole 2x2x4 slice. The times are simulated.
32 devices in a mesh: dp: 16 (over z, x, core), tensor: 2 (over y).
Axes of the slice: x: 2, y: 2, z: 4, core: 2. Of those that a mesh axis runs over, the one named last changes fastest.
Arguments:
- o_inputs: bfloat16 [4096, 8192], P('dp', 'tensor'), may hold values from -6 to 6
- o_gradients: bfloat16 [4096, 8192], P('dp', 'tensor'), may hold values from -6 to 6
- up_inputs: bfloat16 [4096, 8192], P('dp', 'tensor'), may hold values from -6 to 6
- up_gradients: bfloat16 [4096, 28672], P('dp', 'tensor'), may hold values from -6 to 6
- o_in_proj: bfloat16 [8192, 32], P('tensor'), may hold values from -0.0625 to 0.0625
- o_out_proj: bfloat16 [8192, 32], P('tensor'), may hold values from -0.0625 to 0.0625
- up_in_proj: bfloat16 [8192, 32], P('tensor'), may hold values from -0.0625 to 0.0625
- up_out_proj: bfloat16 [28672, 32], P('tensor'), may hold values from -0.03125 to 0.03125
- segment_ids: int32 [16, 256], P('dp'), may hold values from 0 to 3, never falling along the last dimension, each value on 1 to 128 neighbouring positions
- owner_map: int32 [16], replicated, may hold values from 0 to 15, each once
Outputs:
- example_vectors: float32 [2, 64, 1024], P(None, 'dp', 'tensor')
- fisher_owned: float32 [16, 128, 1024], P('dp', None, 'tensor')
Inputs may be any that keep to these rules, and one draw needn't show every extreme that they name: `segment_ids`: within each row, ids never fall; each of the 4 ids holds 1 to 128 tokens, and one holds exactly that many. `owner_map`: each block index appears exactly once.
All inputs are finite; a program needn't handle non-finite values.
Results may differ from a plain program's by a relative error of at most 0.0003.
Values sent between devices are 32-bit elements; how exact they have to be, the bound alone decides.
No kernel may reach another device: no remote copies, remote signals or barrier semaphores. Data moves between devices by JAX's collectives and lax.ppermute only.
A program may use at most 64 MiB of HBM per device.

v0:
```python
import jax
import jax.numpy as jnp
from jax import lax
from jax.sharding import PartitionSpec as P

TOK_DEV = 256
EX_DEV = 4


def local_vectors(segments, in_o, out_o, in_up, out_up):
    examples_local = EX_DEV
    onehot = (segments[:, None] == jnp.arange(examples_local, dtype=jnp.int32)[None, :]).astype(
        jnp.float32
    )
    vector_scale = (EX_DEV / TOK_DEV) ** 0.5
    results = []
    for in_low, out_low in ((in_o, out_o), (in_up, out_up)):
        outers = (out_low[:, :, None] * in_low[:, None, :]).reshape(in_low.shape[0], -1)
        summed = jnp.dot(onehot.T, outers, precision=lax.Precision.HIGHEST)
        results.append(summed * vector_scale)
    return jnp.concatenate(results, axis=1)


def shards(
    o_inputs,
    o_gradients,
    up_inputs,
    up_gradients,
    o_in_proj,
    o_out_proj,
    up_in_proj,
    up_out_proj,
    segment_ids,
    owner_map,
):
    tensor_index = lax.axis_index("tensor")
    tensor_count = lax.axis_size("tensor")
    dp_count = lax.axis_size("dp")
    width = o_in_proj.shape[1] * o_out_proj.shape[1]
    col_width = width // tensor_count
    own_rows = 2 * width // dp_count
    examples_total = EX_DEV * dp_count
    segments = segment_ids[0]
    partials = (
        jnp.dot(o_inputs, o_in_proj, preferred_element_type=jnp.float32),
        jnp.dot(o_gradients, o_out_proj, preferred_element_type=jnp.float32),
        jnp.dot(up_inputs, up_in_proj, preferred_element_type=jnp.float32),
        jnp.dot(up_gradients, up_out_proj, preferred_element_type=jnp.float32),
    )
    in_o, out_o, in_up, out_up = lax.psum(
        (partials[0], partials[1], partials[2], partials[3]), "tensor"
    )
    stacked_vectors = local_vectors(segments, in_o, out_o, in_up, out_up)
    examples_local = stacked_vectors.shape[0]
    by_projection = stacked_vectors.reshape(examples_local, 2, width).transpose(1, 0, 2)
    example_vectors = lax.dynamic_slice_in_dim(
        by_projection, tensor_index * col_width, col_width, 2
    )
    block_range = jnp.arange(owner_map.shape[0], dtype=jnp.int32)

    def block_product(source, owner_block):
        row_part = lax.dynamic_slice_in_dim(source, owner_block * own_rows, own_rows, 1)
        projection = owner_block * own_rows // width
        col_part = lax.dynamic_slice_in_dim(
            source, projection * width + tensor_index * col_width, col_width, 1
        )
        return jnp.dot(row_part.T, col_part, precision=lax.Precision.HIGHEST)

    block_count = lax.axis_size("dp") * own_rows // own_rows
    block_ids = jnp.arange(block_count, dtype=jnp.int32)
    matches = block_ids[:, None] == block_range[None, :]
    owners = jnp.sum(jnp.where(matches, owner_map[None, :], 0), axis=1)
    blocks_done = jax.vmap(lambda owner_block: block_product(stacked_vectors, owner_block))(owners)
    fisher_block = lax.psum_scatter(
        blocks_done.reshape(lax.axis_size("dp") * own_rows, col_width) / examples_total,
        "dp",
        scatter_dimension=0,
        tiled=True,
    )
    return (example_vectors, fisher_block[None])


def solution(mesh):
    in_specs = (
        P("dp", "tensor"),
        P("dp", "tensor"),
        P("dp", "tensor"),
        P("dp", "tensor"),
        P("tensor", None),
        P("tensor", None),
        P("tensor", None),
        P("tensor", None),
        P("dp", None),
        P(),
    )
    out_specs = (P(None, "dp", "tensor"), P("dp", None, "tensor"))
    return jax.shard_map(shards, mesh=mesh, in_specs=in_specs, out_specs=out_specs, check_vma=False)
```

profile of v0, /device:TPU:0, one launch (start us, length us, event | category | flops | bytes accessed | tf_op | source)
XLA Modules:
  0.0 173.6 jit_solution(15110783151214144915)
XLA Ops:
  7.2 1.5 copy-done
  8.8 2.4 %fusion.6 = f32[256,32]{0,1:T(8,128)} fusion(bf16[256,4096]{1,0:T(8,128)(2,1)S(1)} %copy-done, bf16[4096,32]{0,1:T(8,128)(2,1)} %param.14), kind=kOutput, calls=%fused_computation.25 | convolution fusion | flops 67108864 | bytes 2392064 | tf_op jit(solution)/shard_map/dot_general | solution.py:45
  11.2 1.3 fusion.5
  12.6 1.4 fusion.8
  13.9 6.0 %fusion.7 = f32[256,32]{0,1:T(8,128)} fusion(bf16[256,14336]{1,0:T(8,128)(2,1)} %param.13, bf16[14336,32]{0,1:T(8,128)(2,1)S(1)} %copy-done.3), kind=kOutput, calls=%fused_computation.26 | convolution fusion | flops 234881024 | bytes 8290304 | tf_op jit(solution)/shard_map/dot_general | solution.py:48
  20.2 24.5 %all-reduce.5.cloned.1.call-done = (f32[256,32]{0,1:T(8,128)}, f32[256,32]{0,1:T(8,128)}, f32[256,32]{0,1:T(8,128)}, f32[256,32]{0,1:T(8,128)}) async-done(((f32[256,32]{0,1:T(8,128)}, f32[256,32]{0,1:T(8,128)}, f32[256,32]{0,1:T(8,128)}, f32[256,32]{0,1:T(8,128)}), (f32[256,32]{0,1:T(8,128)}, f32[256,32]{0,1:T(8,128)}, f32[256,32]{0,1:T(8,128)}, f32[256,32]{0,1:T(8,128)})) %all-reduce.5.cloned.1.call-update) | async-done | bytes 131088 | tf_op jit(solution)/shard_map/psum | solution.py:50
  44.7 1.1 broadcast_multiply_fusion
  45.8 0.6 convolution_multiply_fusion.1
  46.4 0.6 convolution_multiply_fusion.2
  47.0 21.1 %while.3 = (s32[]{:T(128)}, f32[4,2048]{1,0:T(4,128)S(1)}, s32[16,2]{0,1:T(2,128)S(1)}, f32[16,4,512]{2,1,0:T(4,128)S(1)}, s32[]{:T(128)}) while((s32[]{:T(128)}, f32[4,2048]{1,0:T(4,128)S(1)}, s32[16,2]{0,1:T(2,128)S(1)}, f32[16,4,512]{2,1,0:T(4,128)S(1)}, s32[]{:T(128)}) %tuple.36), condition=%wide.while_cond.1, body=%wide.while_body.1.sunk | while | flops 2 | bytes 16489 | solution.py:64
  47.6 0.7 bitcast_dynamic-update-slice_fusion.5
  48.4 0.5 slice.25
  48.9 0.7 bitcast_dynamic-update-slice_fusion.5
  49.7 0.5 slice.25
  50.3 0.7 bitcast_dynamic-update-slice_fusion.5
  51.6 0.7 bitcast_dynamic-update-slice_fusion.5
  52.9 0.7 bitcast_dynamic-update-slice_fusion.5
  54.2 0.7 bitcast_dynamic-update-slice_fusion.5
  55.5 0.7 bitcast_dynamic-update-slice_fusion.5
  56.8 0.7 bitcast_dynamic-update-slice_fusion.5
  58.2 0.7 bitcast_dynamic-update-slice_fusion.5
  59.5 0.7 bitcast_dynamic-update-slice_fusion.5
  60.8 0.7 bitcast_dynamic-update-slice_fusion.5
  62.1 0.7 bitcast_dynamic-update-slice_fusion.5
  63.4 0.7 bitcast_dynamic-update-slice_fusion.5
  64.7 0.7 bitcast_dynamic-update-slice_fusion.5
  66.1 0.7 bitcast_dynamic-update-slice_fusion.5
  67.4 0.7 bitcast_dynamic-update-slice_fusion.5
  68.1 21.1 %while.2 = (s32[]{:T(128)}, f32[4,2048]{1,0:T(4,128)S(1)}, s32[16,2]{0,1:T(2,128)S(1)}, f32[16,4,128]{2,1,0:T(4,128)S(1)}, s32[]{:T(128)}) while((s32[]{:T(128)}, f32[4,2048]{1,0:T(4,128)S(1)}, s32[16,2]{0,1:T(2,128)S(1)}, f32[16,4,128]{2,1,0:T(4,128)S(1)}, s32[]{:T(128)}) %tuple.44), condition=%wide.while_cond, body=%wide.while_body.sunk | while | flops 2 | bytes 4201 | solution.py:62
  68.7 0.7 bitcast_dynamic-update-slice_fusion.4
  70.0 0.7 bitcast_dynamic-update-slice_fusion.4
  71.3 0.7 bitcast_dynamic-update-slice_fusion.4
  72.6 0.7 bitcast_dynamic-update-slice_fusion.4
  74.0 0.7 bitcast_dynamic-update-slice_fusion.4
  75.3 0.7 bitcast_dynamic-update-slice_fusion.4
  76.6 0.7 bitcast_dynamic-update-slice_fusion.4
  77.9 0.7 bitcast_dynamic-update-slice_fusion.4
  79.2 0.7 bitcast_dynamic-update-slice_fusion.4
  80.5 0.7 bitcast_dynamic-update-slice_fusion.4
  81.9 0.7 bitcast_dynamic-update-slice_fusion.4
  83.2 0.7 bitcast_dynamic-update-slice_fusion.4
  84.5 0.7 bitcast_dynamic-update-slice_fusion.4
  85.8 0.7 bitcast_dynamic-update-slice_fusion.4
  87.1 0.7 bitcast_dynamic-update-slice_fusion.4
  88.4 0.7 bitcast_dynamic-update-slice_fusion.4
  89.2 5.0 %convolution_multiply_fusion = f32[16,128,512]{2,1,0:T(8,128)} fusion(f32[16,4,128]{2,1,0:T(4,128)S(1)} %get-tuple-element.9, f32[16,4,512]{2,1,0:T(4,128)S(1)} %get-tuple-element.17), kind=kOutput, calls=%fused_computation.4 | convolution fusion | flops 51380224 | bytes 4358144 | tf_op jit(solution)/shard_map/vmap()/dot_general | solution.py:67
  94.2 0.6 dynamic-slice_bitcast_fusion
  94.8 71.9 %reduce-scatter.2.cloned.1.call-done = f32[128,512]{1,0:T(8,128)} async-done(((f32[2048,512]{1,0:T(8,128)}), f32[128,512]{1,0:T(8,128)}) %reduce-scatter.2.cloned.1.call-update) | async-done | bytes 262160 | tf_op jit(solution)/shard_map/reduce_scatter | solution.py:74
  (88 shorter events, 18.1 us)
Async XLA Ops:
  7.2 1.6 copy-start
  7.2 4.0 %copy-start.4 = (bf16[4096,32]{0,1:T(8,128)(2,1)S(1)}, bf16[4096,32]{0,1:T(8,128)(2,1)}, u32[]{:S(2)}) copy-start(bf16[4096,32]{0,1:T(8,128)(2,1)} %param.15) | copy-start | bytes 786436
  7.2 37.5 %all-reduce.5.cloned.1.call-start = ((), (), s32[]{:S(2)}) async-start(), calls=%async_computation.2 | async-start | bytes 262144 | tf_op jit(solution)/shard_map/psum | solution.py:50
  8.8 2.5 %copy-start.1 = (bf16[256,4096]{1,0:T(8,128)(2,1)S(1)}, bf16[256,4096]{1,0:T(8,128)(2,1)}, u32[]{:S(2)}) copy-start(bf16[256,4096]{1,0:T(8,128)(2,1)} %param.11) | copy-start | bytes 6291460
  8.8 3.8 %copy-start.2 = (bf16[256,4096]{1,0:T(8,128)(2,1)S(1)}, bf16[256,4096]{1,0:T(8,128)(2,1)}, u32[]{:S(2)}) copy-start(bf16[256,4096]{1,0:T(8,128)(2,1)} %param.12) | copy-start | bytes 6291460
  8.8 3.8 %copy-start.5 = (bf16[4096,32]{0,1:T(8,128)(2,1)S(1)}, bf16[4096,32]{0,1:T(8,128)(2,1)}, u32[]{:S(2)}) copy-start(bf16[4096,32]{0,1:T(8,128)(2,1)} %param.16) | copy-start | bytes 786436
  11.2 2.7 %copy-start.3 = (bf16[14336,32]{0,1:T(8,128)(2,1)S(1)}, bf16[14336,32]{0,1:T(8,128)(2,1)}, u32[]{:S(2)}) copy-start(bf16[14336,32]{0,1:T(8,128)(2,1)} %param.17) | copy-start | bytes 2752516
  13.9 6.1 %copy-start.7 = (s32[16]{0:T(128)S(1)}, s32[16]{0:T(128)}, u32[]{:S(2)}) copy-start(s32[16]{0:T(128)} %param.19) | copy-start | bytes 196
  19.9 25.8 %copy-start.6 = (s32[1,256]{1,0:T(1,128)S(1)}, s32[1,256]{1,0:T(1,128)}, u32[]{:S(2)}) copy-start(s32[1,256]{1,0:T(1,128)} %param.18) | copy-start | bytes 3076
  20.0 146.8 %reduce-scatter.2.cloned.1.call-start = ((), (), s32[]{:S(2)}) async-start(), calls=%async_computation.1 | async-start | bytes 4456448 | tf_op jit(solution)/shard_map/reduce_scatter | solution.py:74
Sparse Core Ops, SparseCore 0:
  20.1 24.5 all-reduce.4
  94.3 72.3 reduce-scatter.1
where the time goes:
time: 174 us
  waiting for transfers between devices  96.4 us (55%)
  local copies, waits for them, and re-layouts  44.3 us (25%)
  matrix products  17.4 us (10%)
  between operations  14.1 us (8%)
    reduce_scatter x1, waiting for transfers between devices, shards(): lax.psum_scatter(blocks_done.reshape(lax.axis_size('dp') * own_rows, col_...  71.9 us
    gather x96, local copies, waits for them, and re-layouts  42.1 us
    psum x1, waiting for transfers between devices, shards(): lax.psum((partials[0], partials[1], partials[2], partials[3]), 'tensor')  24.5 us
    dot_general x1, matrix products, shards(): jnp.dot(up_gradients, up_out_proj, preferred_element_type=jnp.float32)  6.01 us
    dot_general x1, matrix products, block_product(): return jnp.dot(row_part.T, col_part, precision=lax.Precision.HIGHEST)  5.04 us
  transfers between devices with their start and end apart: 2, of which 2 were waited for; matrix products, arithmetic and copies ran while one was open for 0% of the time, Pallas kernels for 0%

commit v1 on v0

v1 whole, which is shorter than its diff:
```python
import functools

import jax
import jax.numpy as jnp
from jax import lax
from jax.experimental import pallas as pl
from jax.experimental.pallas import tpu as pltpu
from jax.sharding import PartitionSpec as P

TOK_DEV = 256
EX_DEV = 4
LANES = 128
NT = (((1,), (1,)), ((), ()))
TN = (((0,), (0,)), ((), ()))
VMEM_BYTES = 60 * 2**20
HIGHEST = lax.Precision.HIGHEST


def chunk_plan(widths):
    plan = []
    for which, width in enumerate(widths):
        pieces = max(1, round(width / 4096))
        while width % pieces or (width // pieces) % LANES:
            pieces += 1
        size = width // pieces
        plan += [(which, start, size) for start in range(0, width, size)]
    return plan


def project_kernel(plan, halves, *refs):
    x_hbm, w_hbm, out_ref = refs[0:4], refs[4:8], refs[8]
    x_vmem, w_vmem, x_sem, w_sem = refs[9:13], refs[13:17], refs[17], refs[18]
    w_copies = [pltpu.make_async_copy(w_hbm[i], w_vmem[i], w_sem.at[i]) for i in range(4)]
    x_copies = [
        pltpu.make_async_copy(
            x_hbm[i].at[:, pl.ds(start, size)], x_vmem[i].at[:, pl.ds(start, size)], x_sem.at[n]
        )
        for n, (i, start, size) in enumerate(plan)
    ]
    for n, (i, start, size) in enumerate(plan):
        if start == 0:
            w_copies[i].start()
        x_copies[n].start()
    tokens, rank = x_vmem[0].shape[0], w_vmem[0].shape[0]
    part = tokens // halves
    totals = None
    for n, (i, start, size) in enumerate(plan):
        if start == 0:
            w_copies[i].wait()
        x_copies[n].wait()
        w = w_vmem[i][:, pl.ds(start, size)]
        products = [
            lax.dot_general(
                w, x_vmem[i][pl.ds(h * part, part), pl.ds(start, size)], NT, preferred_element_type=jnp.float32
            )
            for h in range(halves)
        ]
        totals = products if start == 0 else [a + b for a, b in zip(totals, products)]
        if start + size == x_vmem[i].shape[1]:
            for h in range(halves):
                out_ref[pl.ds(i * rank, rank), pl.ds(h * part, part)] = totals[h]


def project(xs, ws):
    plan = chunk_plan([x.shape[1] for x in xs])
    tokens, rank = xs[0].shape[0], ws[0].shape[0]
    return pl.pallas_call(
        functools.partial(project_kernel, plan, 2),
        out_shape=jax.ShapeDtypeStruct((4 * rank, tokens), jnp.float32),
        in_specs=[pl.BlockSpec(memory_space=pl.ANY)] * 8,
        out_specs=pl.BlockSpec(memory_space=pltpu.VMEM),
        scratch_shapes=[pltpu.VMEM(x.shape, x.dtype) for x in xs]
        + [pltpu.VMEM(w.shape, w.dtype) for w in ws]
        + [pltpu.SemaphoreType.DMA((len(plan),)), pltpu.SemaphoreType.DMA((4,))],
        compiler_params=pltpu.CompilerParams(vmem_limit_bytes=VMEM_BYTES),
        name="project",
    )(*xs, *ws)


def vectors_kernel(n_parts, own_rows, *refs):
    parts, seg_ref, owner_ref, vec_ref, send_ref, slabs = refs[:n_parts], *refs[n_parts:]
    low = parts[0][...]
    for other in parts[1:]:
        low = low + other[...]
    rank, tokens = low.shape[0] // 4, low.shape[1]
    fold = LANES // rank
    n_slabs = rank // fold
    col_slabs = vec_ref.shape[2] // LANES
    seg = seg_ref[...]
    rows = EX_DEV * rank
    row = lax.broadcasted_iota(jnp.int32, (rows, LANES), 0)
    lane = lax.broadcasted_iota(jnp.int32, (rows, LANES), 1)
    scale = (EX_DEV / TOK_DEV) ** 0.5
    keep = jnp.where(row % fold == lane // rank, scale, 0.0).astype(jnp.float32)
    to = lax.broadcasted_iota(jnp.int32, (n_slabs * EX_DEV, rows), 0)
    frm = lax.broadcasted_iota(jnp.int32, (n_slabs * EX_DEV, rows), 1)
    gather = (frm // rank == to % EX_DEV) & ((frm % rank) // fold == to // EX_DEV)
    gather = jnp.where(gather, 1.0, 0.0).astype(jnp.float32)
    for p in range(2):
        in_low = low[2 * p * rank : (2 * p + 1) * rank]
        out_low = low[(2 * p + 1) * rank : (2 * p + 2) * rank]
        in_wide = jnp.concatenate([in_low] * fold, axis=0)
        masked = jnp.concatenate([jnp.where(seg == e, out_low, 0.0) for e in range(EX_DEV)], axis=0)
        outer = lax.dot_general(masked, in_wide, NT, precision=HIGHEST, preferred_element_type=jnp.float32)
        flat = jnp.dot(gather, outer * keep, precision=HIGHEST, preferred_element_type=jnp.float32)
        for g in range(n_slabs):
            slabs[p * n_slabs + g] = flat[g * EX_DEV : (g + 1) * EX_DEV]
    t = lax.axis_index("tensor")
    for p in range(2):
        for k in range(col_slabs):
            vec_ref[p, :, pl.ds(k * LANES, LANES)] = slabs[p * n_slabs + t * col_slabs + k]
    for j in range(send_ref.shape[0]):
        first_row = owner_ref[j] * own_rows
        p = first_row // (rank * rank)
        send_ref[j, 0] = slabs[first_row // LANES]
        for k in range(col_slabs):
            send_ref[j, 1 + k] = slabs[p * n_slabs + t * col_slabs + k]


def vectors(parts, segments, owner_map, col_width, own_rows, dp_count):
    n_slabs = (parts[0].shape[0] // 4) ** 2 // LANES
    vmem, smem = pl.BlockSpec(memory_space=pltpu.VMEM), pl.BlockSpec(memory_space=pltpu.SMEM)
    return pl.pallas_call(
        functools.partial(vectors_kernel, len(parts), own_rows),
        out_shape=(
            jax.ShapeDtypeStruct((2, EX_DEV, col_width), jnp.float32),
            jax.ShapeDtypeStruct((dp_count, 1 + col_width // LANES, EX_DEV, LANES), jnp.float32),
        ),
        in_specs=[vmem] * len(parts) + [vmem, smem],
        out_specs=(vmem, vmem),
        scratch_shapes=[pltpu.VMEM((2 * n_slabs, EX_DEV, LANES), jnp.float32)],
        name="vectors",
    )(*parts, segments, owner_map)


def fisher_kernel(scale, recv_ref, owner_ref, out_ref, stack, full):
    count, slabs = recv_ref.shape[0], recv_ref.shape[1]
    for i in range(count):
        for k in range(slabs):
            stack[pl.ds(i * EX_DEV, EX_DEV), pl.ds(k * LANES, LANES)] = recv_ref[i, k]
    product = lax.dot_general(
        stack[:, pl.ds(0, LANES)],
        stack[:, pl.ds(LANES, (slabs - 1) * LANES)],
        TN,
        precision=HIGHEST,
        preferred_element_type=jnp.float32,
    )
    own_rows = out_ref.shape[1]
    if own_rows == LANES:
        out_ref[0] = product * scale
    else:
        full[...] = product * scale
        start = (owner_ref[lax.axis_index("dp")] * own_rows) % LANES
        out_ref[0] = full[pl.ds(pl.multiple_of(start, own_rows), own_rows), :]


def fisher(recv, owner_map, own_rows):
    count, slabs = recv.shape[:2]
    col_width = (slabs - 1) * LANES
    return pl.pallas_call(
        functools.partial(fisher_kernel, 1.0 / (EX_DEV * count)),
        out_shape=jax.ShapeDtypeStruct((1, own_rows, col_width), jnp.float32),
        in_specs=[pl.BlockSpec(memory_space=pltpu.VMEM), pl.BlockSpec(memory_space=pltpu.SMEM)],
        out_specs=pl.BlockSpec(memory_space=pltpu.VMEM),
        scratch_shapes=[
            pltpu.VMEM((EX_DEV * count, slabs * LANES), jnp.float32),
            pltpu.VMEM((LANES, col_width), jnp.float32),
        ],
        name="fisher",
    )(recv, owner_map)


def shards(
    o_inputs,
    o_gradients,
    up_inputs,
    up_gradients,
    o_in_proj,
    o_out_proj,
    up_in_proj,
    up_out_proj,
    segment_ids,
    owner_map,
):
    tensor_count = lax.axis_size("tensor")
    dp_count = lax.axis_size("dp")
    width = o_in_proj.shape[1] * o_out_proj.shape[1]
    col_width = width // tensor_count
    own_rows = 2 * width // dp_count
    partial = project(
        (o_inputs, o_gradients, up_inputs, up_gradients),
        (o_in_proj.T, o_out_proj.T, up_in_proj.T, up_out_proj.T),
    )
    if tensor_count == 2:
        parts = (partial, lax.ppermute(partial, "tensor", [(0, 1), (1, 0)]))
    else:
        parts = (lax.psum(partial, "tensor"),)
    example_vectors, send = vectors(parts, segment_ids, owner_map, col_width, own_rows, dp_count)
    recv = lax.all_to_all(send, "dp", 0, 0, tiled=True)
    return example_vectors, fisher(recv, owner_map, own_rows)


def solution(mesh):
    in_specs = (
        P("dp", "tensor"),
        P("dp", "tensor"),
        P("dp", "tensor"),
        P("dp", "tensor"),
        P("tensor", None),
        P("tensor", None),
        P("tensor", None),
        P("tensor", None),
        P("dp", None),
        P(),
    )
    out_specs = (P(None, "dp", "tensor"), P("dp", None, "tensor"))
    return jax.shard_map(shards, mesh=mesh, in_specs=in_specs, out_specs=out_specs, check_vma=False)
```

time: 174 us -> 36.4 us (0.21)
  waiting for transfers between devices: 96.4 us -> 3.7 us
  local copies, waits for them, and re-layouts: 44.3 us -> 0.64 us
  matrix products: 17.4 us -> 0 us
  blocking collectives: 0 us -> 14.7 us
  between operations: 14.1 us -> 0.64 us
  Pallas kernels: 0 us -> 13.4 us
  starting transfers between devices: 0.08 us -> 3.03 us
    reduce_scatter x1 -> x0, waiting for transfers between devices: 71.9 us -> none  [shards(): lax.psum_scatter(blocks_done.reshape(lax.axis_size('dp') * own_rows, col_...]
    gather x96 -> x0, local copies, waits for them, and re-layouts: 42.1 us -> none
    psum x1 -> x0, waiting for transfers between devices: 24.5 us -> none  [shards(): lax.psum((partials[0], partials[1], partials[2], partials[3]), 'tensor')]
    dot_general x7 -> x0, matrix products: 17.4 us -> none  [the longest x1 6.01 us: shards(): jnp.dot(up_gradients, up_out_proj, preferred_element_type=jnp.float32)]
    all_to_all x0 -> x1, blocking collectives: none -> 14.7 us  [shards(): recv = lax.all_to_all(send, 'dp', 0, 0, tiled=True)]
    pallas_call x0 -> x3, Pallas kernels: none -> 13.4 us  [the longest x1 8.65 us: project(): pl.pallas_call(functools.partial(project_kernel, plan, 2), out_shape=jax....]
    ppermute x0 -> x1, waiting for transfers between devices: none -> 3.7 us  [shards(): parts = (partial, lax.ppermute(partial, 'tensor', [(0, 1), (1, 0)]))]
    ppermute x0 -> x1, starting transfers between devices: none -> 3.03 us  [shards(): parts = (partial, lax.ppermute(partial, 'tensor', [(0, 1), (1, 0)]))]
  transfers between devices with their start and end apart: 2 -> 1, of which waited for: 2 -> 1; matrix products, arithmetic and copies ran while one was open for 0% -> 0% of each run, Pallas kernels for 0% -> 0%
where the time goes in v1:
time: 36.4 us; the launch traced here: 36.2 us
  blocking collectives  14.7 us (40%)
  Pallas kernels  13.4 us (37%)
  waiting for transfers between devices  3.7 us (10%)
  starting transfers between devices  3.03 us (8%)
  local copies, waits for them, and re-layouts  0.64 us (2%)
  between operations  0.64 us (2%)
    all_to_all x1, blocking collectives, shards(): recv = lax.all_to_all(send, 'dp', 0, 0, tiled=True)  14.7 us
    pallas_call x1, Pallas kernels, project(): pl.pallas_call(functools.partial(project_kernel, plan, 2), out_shape=jax....  8.65 us
    ppermute x1, waiting for transfers between devices, shards(): parts = (partial, lax.ppermute(partial, 'tensor', [(0, 1), (1, 0)]))  3.7 us
    ppermute x1, starting transfers between devices, shards(): parts = (partial, lax.ppermute(partial, 'tensor', [(0, 1), (1, 0)]))  3.03 us
    pallas_call x1, Pallas kernels, vectors(): pl.pallas_call(functools.partial(vectors_kernel, len(parts), own_rows), o...  2.72 us
    pallas_call x1, Pallas kernels, fisher(): pl.pallas_call(functools.partial(fisher_kernel, 1.0 / (EX_DEV * count)),...  2.06 us
  transfers between devices with their start and end apart: 1, of which 1 were waited for; matrix products, arithmetic and copies ran while one was open for 0% of the time, Pallas kernels for 0%

profile of v1, /device:TPU:0, one launch (start us, length us, event | category | flops | bytes accessed | tf_op | source)
XLA Modules:
  0.0 36.2 jit_solution(16821856626699738352)
XLA Ops:
  0.6 8.6 %project.1.refs_0_ = f32[128,256]{1,0:T(8,128)} custom-call(bf16[256,4096]{1,0:T(8,128)(2,1)} %refs_0_.1, bf16[256,4096]{1,0:T(8,128)(2,1)} %refs_1_.1, bf16[256,4096]{1,0:T(8,128)(2,1)} %refs_2_.2, bf16[256,14336]{1,0:T(8,128)(2,1)} %refs_3_.2, bf16[32,4096]{1,0:T(8,128)(2,1)} %bitcast.5, bf16[32,4096]{1,0:T(8,128)(2,1)} %bitcast.6, ...), custom_call_target="tpu_custom_call" | custom-call | tf_op jit(solution)/shard_map/project/pallas_call | solution.py:67
  9.3 3.0 %collective-permute-start = (f32[128,256]{1,0:T(8,128)}, f32[128,256]{1,0:T(8,128)S(1)}, u32[]{:S(2)}, u32[]{:S(2)}) collective-permute-start(f32[128,256]{1,0:T(8,128)} %project.1.refs_0_), channel_id=1, source_target_pairs={{0,1},{1,0},{2,3},{3,2},{4,5},{5,4},{6,7},{7,6},{8,9},{9,8},{10,11... | collective-permute-start | bytes 393224 | tf_op jit(solution)/shard_map/ppermute | solution.py:195
  12.3 3.7 %collective-permute-done.refs_1_ = f32[128,256]{1,0:T(8,128)S(1)} collective-permute-done((f32[128,256]{1,0:T(8,128)}, f32[128,256]{1,0:T(8,128)S(1)}, u32[]{:S(2)}, u32[]{:S(2)}) %collective-permute-start) | collective-permute-done | bytes 131104 | tf_op jit(solution)/shard_map/ppermute | solution.py:195
  16.0 0.0 copy-start
  16.0 0.6 %copy-done = f32[128,256]{1,0:T(8,128)} copy-done((f32[128,256]{1,0:T(8,128)}, f32[128,256]{1,0:T(8,128)S(1)}, u32[]{:S(2)}) %copy-start) | copy-done | bytes 131096
  16.7 2.7 %vectors.1 = (f32[2,4,512]{2,1,0:T(4,128)}, f32[16,5,4,128]{3,2,1,0:T(4,128)}) custom-call(f32[128,256]{1,0:T(8,128)} %project.1.refs_0_, f32[128,256]{1,0:T(8,128)} %copy-done, s32[1,256]{1,0:T(1,128)} %refs_2_.3, s32[16]{0:T(128)} %owner_ref.1), custom_call_target="tpu_custom_call" | custom-call | tf_op jit(solution)/shard_map/vectors/pallas_call | solution.py:123
  19.4 14.7 %all_to_all.5.recv_ref = f32[16,5,4,128]{3,2,1,0:T(4,128)} all-to-all(f32[16,5,4,128]{3,2,1,0:T(4,128)} %get-tuple-element.5), channel_id=1, replica_groups=mesh['dp'=16,'tensor'=2] {'dp'}, dimensions={0} | all-to-all | bytes 327680 | tf_op jit(solution)/shard_map/all_to_all | solution.py:199
  34.1 2.1 %fisher.1 = f32[1,128,512]{2,1,0:T(8,128)} custom-call(f32[16,5,4,128]{3,2,1,0:T(4,128)} %all_to_all.5.recv_ref, s32[16]{0:T(128)} %owner_ref.1), custom_call_target="tpu_custom_call" | custom-call | tf_op jit(solution)/shard_map/fisher/pallas_call | solution.py:160
Async XLA Ops:
  9.3 6.7 %collective-permute-start = (f32[128,256]{1,0:T(8,128)}, f32[128,256]{1,0:T(8,128)S(1)}, u32[]{:S(2)}, u32[]{:S(2)}) collective-permute-start(f32[128,256]{1,0:T(8,128)} %project.1.refs_0_), channel_id=1, source_target_pairs={{0,1},{1,0},{2,3},{3,2},{4,5},{5,4},{6,7},{7,6},{8,9},{9,8},{10,11... | collective-permute-start | bytes 393224 | tf_op jit(solution)/shard_map/ppermute | solution.py:195
  16.0 0.6 %copy-start = (f32[128,256]{1,0:T(8,128)}, f32[128,256]{1,0:T(8,128)S(1)}, u32[]{:S(2)}) copy-start(f32[128,256]{1,0:T(8,128)S(1)} %collective-permute-done.refs_1_) | copy-start | bytes 393220

commit v2 on v1

v2 whole, which is shorter than its diff:
```python
import functools

import jax
import jax.numpy as jnp
from jax import lax
from jax.experimental import pallas as pl
from jax.experimental.pallas import tpu as pltpu
from jax.sharding import PartitionSpec as P

TOK_DEV = 256
EX_DEV = 4
LANES = 128
NT = (((1,), (1,)), ((), ()))
TN = (((0,), (0,)), ((), ()))
VMEM_BYTES = 60 * 2**20
SMALL_BYTES = 8 * 2**20


def chunk_plan(widths):
    plan = []
    for which in sorted(range(len(widths)), key=lambda i: -widths[i]):
        start = 0
        while start < widths[which]:
            left = widths[which] - start
            size = left if left <= 6144 else 4096
            plan.append((which, start, size))
            start += size
    return plan


def split(x):
    high = x.astype(jnp.bfloat16)
    return high, (x - high.astype(jnp.float32)).astype(jnp.bfloat16)


def project_kernel(plan, halves, *refs):
    x_hbm, w_hbm, outs = refs[0:4], refs[4:8], refs[8:9]
    x_vmem, w_vmem, x_sem, w_sem = refs[9:13], refs[13:17], refs[17], refs[18]
    w_copies = [pltpu.make_async_copy(w_hbm[i], w_vmem[i], w_sem.at[i]) for i in range(4)]
    x_copies = [
        pltpu.make_async_copy(
            x_hbm[i].at[:, pl.ds(start, size)], x_vmem[i].at[:, pl.ds(start, size)], x_sem.at[n]
        )
        for n, (i, start, size) in enumerate(plan)
    ]
    for n, (i, start, size) in enumerate(plan):
        if start == 0:
            w_copies[i].start()
        x_copies[n].start()
    tokens, rank = x_vmem[0].shape[0], w_vmem[0].shape[0]
    part = tokens // halves
    totals = {}
    for n, (i, start, size) in enumerate(plan):
        if start == 0:
            w_copies[i].wait()
        x_copies[n].wait()
        w = w_vmem[i][:, pl.ds(start, size)]
        for h in range(halves):
            x = x_vmem[i][pl.ds(h * part, part), pl.ds(start, size)]
            product = lax.dot_general(x, w, NT, preferred_element_type=jnp.float32)
            totals[i, h] = product if start == 0 else totals[i, h] + product
    for i in range(4):
        for h in range(halves):
            low = totals[i, h].T
            for out in outs:
                out[h, pl.ds(i * rank, rank), :] = low


def project(xs, ws):
    plan = chunk_plan([x.shape[1] for x in xs])
    tokens, rank = xs[0].shape[0], ws[0].shape[0]
    halves = tokens // LANES
    low = jax.ShapeDtypeStruct((halves, 4 * rank, LANES), jnp.float32)
    return pl.pallas_call(
        functools.partial(project_kernel, plan, halves),
        out_shape=(low,),
        in_specs=[pl.BlockSpec(memory_space=pl.ANY)] * 8,
        out_specs=(pl.BlockSpec(memory_space=pltpu.VMEM),),
        scratch_shapes=[pltpu.VMEM(x.shape, x.dtype) for x in xs]
        + [pltpu.VMEM(w.shape, w.dtype) for w in ws]
        + [pltpu.SemaphoreType.DMA((len(plan),)), pltpu.SemaphoreType.DMA((4,))],
        compiler_params=pltpu.CompilerParams(vmem_limit_bytes=VMEM_BYTES),
        name="project",
    )(*xs, *ws)


def stage_kernel(low_ref, out_ref):
    out_ref[...] = low_ref[...]


def stage(low):
    return pl.pallas_call(
        stage_kernel,
        out_shape=jax.ShapeDtypeStruct(low.shape, low.dtype),
        in_specs=[pl.BlockSpec(memory_space=pltpu.VMEM)],
        out_specs=pl.BlockSpec(memory_space=pltpu.VMEM),
        compiler_params=pltpu.CompilerParams(vmem_limit_bytes=SMALL_BYTES),
        name="stage",
    )(low)


def vectors_kernel(n_parts, own_rows, *refs):
    parts, seg_ref, owner_ref, vec_ref, send_ref, slabs = refs[:n_parts], *refs[n_parts:]
    halves, rank = parts[0].shape[0], parts[0].shape[1] // 4
    fold = LANES // rank
    n_slabs = rank // fold
    col_slabs = vec_ref.shape[2] // LANES
    seg = seg_ref[...]
    lane = lax.broadcasted_iota(jnp.int32, (EX_DEV * n_slabs, LANES), 1)
    scale = (EX_DEV / TOK_DEV) ** 0.5

    def total(index):
        sums = [functools.reduce(lambda a, b: a + b, [part[h, index, :] for part in parts]) for h in range(halves)]
        return jnp.concatenate(sums, axis=1)

    for p in range(2):
        in_high, in_low = split(total(pl.ds(2 * p * rank, rank)))
        in_wide = jnp.concatenate([in_high, in_low, in_high], axis=1)
        in_wide = jnp.concatenate([in_wide] * fold, axis=0)
        rows = []
        for b in range(fold):
            out_rows = total(pl.ds((2 * p + 1) * rank + b, n_slabs, stride=fold))
            rows += [jnp.where(seg == e, out_rows, 0.0) for e in range(EX_DEV)]
        out_high, out_low = split(jnp.concatenate(rows, axis=0))
        out_wide = jnp.concatenate([out_high, out_high, out_low], axis=1)
        outer = lax.dot_general(out_wide, in_wide, NT, preferred_element_type=jnp.float32)
        flat = outer[: EX_DEV * n_slabs]
        for b in range(1, fold):
            block = outer[b * EX_DEV * n_slabs : (b + 1) * EX_DEV * n_slabs]
            flat = jnp.where(lane // rank == b, block, flat)
        flat = flat * scale
        for g in range(n_slabs):
            slabs[p * n_slabs + g] = jnp.concatenate(
                [flat[e * n_slabs + g : e * n_slabs + g + 1] for e in range(EX_DEV)], axis=0
            )
    t = lax.axis_index("tensor")
    for p in range(2):
        for k in range(col_slabs):
            vec_ref[p, :, pl.ds(k * LANES, LANES)] = slabs[p * n_slabs + t * col_slabs + k]
    for j in range(send_ref.shape[0]):
        first_row = owner_ref[j] * own_rows
        p = first_row // (rank * rank)
        send_ref[j, 0] = slabs[first_row // LANES]
        for k in range(col_slabs):
            send_ref[j, 1 + k] = slabs[p * n_slabs + t * col_slabs + k]


def vectors(parts, segments, owner_map, col_width, own_rows, dp_count):
    n_slabs = (parts[0].shape[1] // 4) ** 2 // LANES
    vmem, smem = pl.BlockSpec(memory_space=pltpu.VMEM), pl.BlockSpec(memory_space=pltpu.SMEM)
    return pl.pallas_call(
        functools.partial(vectors_kernel, len(parts), own_rows),
        out_shape=(
            jax.ShapeDtypeStruct((2, EX_DEV, col_width), jnp.float32),
            jax.ShapeDtypeStruct((dp_count, 1 + col_width // LANES, EX_DEV, LANES), jnp.float32),
        ),
        in_specs=[vmem] * len(parts) + [vmem, smem],
        out_specs=(vmem, vmem),
        scratch_shapes=[pltpu.VMEM((2 * n_slabs, EX_DEV, LANES), jnp.float32)],
        compiler_params=pltpu.CompilerParams(vmem_limit_bytes=SMALL_BYTES),
        name="vectors",
    )(*parts, segments, owner_map)


def fisher_kernel(scale, recv_ref, vec_ref, owner_ref, out_ref, vec_out, stack, full, sems):
    store = pltpu.make_async_copy(vec_ref, vec_out, sems.at[0])
    store.start()
    count, slabs = recv_ref.shape[0], recv_ref.shape[1]
    for i in range(count):
        for k in range(slabs):
            stack[pl.ds(i * EX_DEV, EX_DEV), pl.ds(k * LANES, LANES)] = recv_ref[i, k]
    own_rows, col_width = out_ref.shape[1:]
    start = 0
    if own_rows < LANES:
        start = (owner_ref[lax.axis_index("dp")] * own_rows) % LANES
        start = pl.multiple_of(start, own_rows)
    row_high, row_low = split(stack[:, pl.ds(0, LANES)])
    row_wide = jnp.concatenate([row_high, row_high, row_low], axis=0)
    pieces = 2 if col_width % (2 * LANES) == 0 else 1
    size = col_width // pieces
    stores = [store]
    for c in range(pieces):
        col_high, col_low = split(stack[:, pl.ds(LANES + c * size, size)])
        col_wide = jnp.concatenate([col_high, col_low, col_high], axis=0)
        product = lax.dot_general(row_wide, col_wide, TN, preferred_element_type=jnp.float32)
        full[:, pl.ds(c * size, size)] = product * scale
        stores.append(
            pltpu.make_async_copy(
                full.at[pl.ds(start, own_rows), pl.ds(c * size, size)],
                out_ref.at[0, :, pl.ds(c * size, size)],
                sems.at[1 + c],
            )
        )
        stores[-1].start()
    for store in stores:
        store.wait()


def fisher(recv, vec, owner_map, own_rows):
    count, slabs = recv.shape[:2]
    col_width = (slabs - 1) * LANES
    hbm = pl.BlockSpec(memory_space=pl.ANY)
    return pl.pallas_call(
        functools.partial(fisher_kernel, 1.0 / (EX_DEV * count)),
        out_shape=(
            jax.ShapeDtypeStruct((1, own_rows, col_width), jnp.float32),
            jax.ShapeDtypeStruct(vec.shape, vec.dtype),
        ),
        in_specs=[pl.BlockSpec(memory_space=pltpu.VMEM), hbm, pl.BlockSpec(memory_space=pltpu.SMEM)],
        out_specs=(hbm, hbm),
        scratch_shapes=[
            pltpu.VMEM((EX_DEV * count, slabs * LANES), jnp.float32),
            pltpu.VMEM((LANES, col_width), jnp.float32),
            pltpu.SemaphoreType.DMA((3,)),
        ],
        compiler_params=pltpu.CompilerParams(vmem_limit_bytes=SMALL_BYTES),
        name="fisher",
    )(recv, vec, owner_map)


def shards(
    o_inputs,
    o_gradients,
    up_inputs,
    up_gradients,
    o_in_proj,
    o_out_proj,
    up_in_proj,
    up_out_proj,
    segment_ids,
    owner_map,
):
    tensor_count = lax.axis_size("tensor")
    dp_count = lax.axis_size("dp")
    width = o_in_proj.shape[1] * o_out_proj.shape[1]
    col_width = width // tensor_count
    own_rows = 2 * width // dp_count
    (own,) = project(
        (o_inputs, o_gradients, up_inputs, up_gradients),
        (o_in_proj.T, o_out_proj.T, up_in_proj.T, up_out_proj.T),
    )
    if tensor_count == 2:
        parts = (stage(own), lax.ppermute(own, "tensor", [(0, 1), (1, 0)]))
    else:
        parts = (lax.psum(own, "tensor"),)
    vec, send = vectors(parts, segment_ids, owner_map, col_width, own_rows, dp_count)
    recv = lax.all_to_all(send, "dp", 0, 0, tiled=True)
    fisher_block, example_vectors = fisher(recv, vec, owner_map, own_rows)
    return example_vectors, fisher_block


def solution(mesh):
    in_specs = (
        P("dp", "tensor"),
        P("dp", "tensor"),
        P("dp", "tensor"),
        P("dp", "tensor"),
        P("tensor", None),
        P("tensor", None),
        P("tensor", None),
        P("tensor", None),
        P("dp", None),
        P(),
    )
    out_specs = (P(None, "dp", "tensor"), P("dp", None, "tensor"))
    return jax.shard_map(shards, mesh=mesh, in_specs=in_specs, out_specs=out_specs, check_vma=False)
```

time: 36.4 us -> 31.9 us (0.88)
  Pallas kernels: 13.4 us -> 9.93 us
  waiting for transfers between devices: 3.7 us -> 2.76 us
    pallas_call x1, Pallas kernels: 2.72 us -> 0.91 us  [vectors(): pl.pallas_call(functools.partial(vectors_kernel, len(parts), own_rows), o...]
    pallas_call x1 -> x2, Pallas kernels: 8.65 us -> 7.53 us  [the longest x1 7.52 us: project(): pl.pallas_call(functools.partial(project_kernel, plan, halves), out_shape...]
    ppermute x1, waiting for transfers between devices: 3.7 us -> 2.76 us  [shards(): parts = (stage(own), lax.ppermute(own, 'tensor', [(0, 1), (1, 0)]))]
    pallas_call x1, Pallas kernels: 2.06 us -> 1.49 us  [fisher(): pl.pallas_call(functools.partial(fisher_kernel, 1.0 / (EX_DEV * count)),...]
    unnamed x2 -> x6, local copies, waits for them, and re-layouts: 0.64 us -> 0.95 us
where the time goes in v2:
time: 31.9 us; the launch traced here: 31.7 us
  blocking collectives  14.4 us (45%)
  Pallas kernels  9.93 us (31%)
  starting transfers between devices  3.03 us (9%)
  waiting for transfers between devices  2.76 us (9%)
  local copies, waits for them, and re-layouts  0.95 us (3%)
  between operations  0.67 us (2%)
    all_to_all x1, blocking collectives, shards(): recv = lax.all_to_all(send, 'dp', 0, 0, tiled=True)  14.4 us
    pallas_call x1, Pallas kernels, project(): pl.pallas_call(functools.partial(project_kernel, plan, halves), out_shape...  7.52 us
    ppermute x1, starting transfers between devices, shards(): parts = (stage(own), lax.ppermute(own, 'tensor', [(0, 1), (1, 0)]))  3.03 us
    ppermute x1, waiting for transfers between devices, shards(): parts = (stage(own), lax.ppermute(own, 'tensor', [(0, 1), (1, 0)]))  2.76 us
    pallas_call x1, Pallas kernels, fisher(): pl.pallas_call(functools.partial(fisher_kernel, 1.0 / (EX_DEV * count)),...  1.49 us
    unnamed x6, local copies, waits for them, and re-layouts  0.95 us
    pallas_call x1, Pallas kernels, vectors(): pl.pallas_call(functools.partial(vectors_kernel, len(parts), own_rows), o...  0.91 us
  transfers between devices with their start and end apart: 1, of which 1 were waited for; matrix products, arithmetic and copies ran while one was open for 0% of the time, Pallas kernels for 0%

profile of v2, /device:TPU:0, one launch (start us, length us, event | category | flops | bytes accessed | tf_op | source)
XLA Modules:
  0.0 31.7 jit_solution(7042960606235404756)
XLA Ops:
  0.6 0.0 copy-start.1
  0.6 0.0 copy-start.2
  0.7 7.5 %project.1.low_ref = f32[2,128,128]{2,1,0:T(8,128)} custom-call(bf16[256,4096]{1,0:T(8,128)(2,1)} %refs_0_.1, bf16[256,4096]{1,0:T(8,128)(2,1)} %refs_1_.1, bf16[256,4096]{1,0:T(8,128)(2,1)} %refs_2_.2, bf16[256,14336]{1,0:T(8,128)(2,1)} %refs_3_.2, bf16[32,4096]{1,0:T(8,128)(2,1)} %bitcast.5, bf16[32,4096]{1,0:T(8,128)(2,1)} %bitcast.6, ...), custom_call_target="tpu_custom_call" | custom-call | tf_op jit(solution)/shard_map/project/pallas_call | solution.py:74
  8.2 3.0 %collective-permute-start = (f32[2,128,128]{2,1,0:T(8,128)}, f32[2,128,128]{2,1,0:T(8,128)S(1)}, u32[]{:S(2)}, u32[]{:S(2)}) collective-permute-start(f32[2,128,128]{2,1,0:T(8,128)} %project.1.low_ref), channel_id=1, source_target_pairs={{0,1},{1,0},{2,3},{3,2},{4,5},{5,4},{6,7},{7,6},{8,9},{9,8},{10,11... | collective-permute-start | bytes 393224 | tf_op jit(solution)/shard_map/ppermute | solution.py:243
  11.2 0.0 copy-start
  11.2 0.9 %copy-done = f32[2,128,128]{2,1,0:T(8,128)S(1)} copy-done((f32[2,128,128]{2,1,0:T(8,128)S(1)}, f32[2,128,128]{2,1,0:T(8,128)}, u32[]{:S(2)}) %copy-start) | copy-done | bytes 131096
  12.2 2.8 %collective-permute-done.refs_1_ = f32[2,128,128]{2,1,0:T(8,128)S(1)} collective-permute-done((f32[2,128,128]{2,1,0:T(8,128)}, f32[2,128,128]{2,1,0:T(8,128)S(1)}, u32[]{:S(2)}, u32[]{:S(2)}) %collective-permute-start) | collective-permute-done | bytes 131104 | tf_op jit(solution)/shard_map/ppermute | solution.py:243
  14.9 0.0 copy-done.1
  14.9 0.0 copy-done.2
  14.9 0.9 %vectors.1 = (f32[2,4,512]{2,1,0:T(4,128)S(1)}, f32[16,5,4,128]{3,2,1,0:T(4,128)S(1)}) custom-call(f32[2,128,128]{2,1,0:T(8,128)S(1)} %stage.1.refs_0_, f32[2,128,128]{2,1,0:T(8,128)S(1)} %collective-permute-done.refs_1_, s32[1,256]{1,0:T(1,128)S(1)} %copy-done.2, s32[16]{0:T(128)S(1)} %copy-done.1), custom_call_target="tpu_custom_call" | custom-call | tf_op jit(solution)/shard_map/vectors/pallas_call | solution.py:151
  15.8 14.4 %all_to_all.5.recv_ref = f32[16,5,4,128]{3,2,1,0:T(4,128)S(1)} all-to-all(f32[16,5,4,128]{3,2,1,0:T(4,128)S(1)} %get-tuple-element.6), channel_id=1, replica_groups=mesh['dp'=16,'tensor'=2] {'dp'}, dimensions={0} | all-to-all | bytes 327680 | tf_op jit(solution)/shard_map/all_to_all | solution.py:247
  30.2 1.5 %fisher.1 = (f32[1,128,512]{2,1,0:T(8,128)}, f32[2,4,512]{2,1,0:T(4,128)}) custom-call(f32[16,5,4,128]{3,2,1,0:T(4,128)S(1)} %all_to_all.5.recv_ref, f32[2,4,512]{2,1,0:T(4,128)S(1)} %get-tuple-element.7.vec_ref, s32[16]{0:T(128)S(1)} %copy-done.1), custom_call_target="tpu_custom_call" | custom-call | tf_op jit(solution)/shard_map/fisher/pallas_call | solution.py:203
  (1 shorter events, 0.0 us)
Async XLA Ops:
  0.6 14.3 %copy-start.1 = (s32[16]{0:T(128)S(1)}, s32[16]{0:T(128)}, u32[]{:S(2)}) copy-start(s32[16]{0:T(128)} %owner_ref.1) | copy-start | bytes 196
  0.6 14.3 %copy-start.2 = (s32[1,256]{1,0:T(1,128)S(1)}, s32[1,256]{1,0:T(1,128)}, u32[]{:S(2)}) copy-start(s32[1,256]{1,0:T(1,128)} %refs_2_.3) | copy-start | bytes 3076
  8.2 6.7 %collective-permute-start = (f32[2,128,128]{2,1,0:T(8,128)}, f32[2,128,128]{2,1,0:T(8,128)S(1)}, u32[]{:S(2)}, u32[]{:S(2)}) collective-permute-start(f32[2,128,128]{2,1,0:T(8,128)} %project.1.low_ref), channel_id=1, source_target_pairs={{0,1},{1,0},{2,3},{3,2},{4,5},{5,4},{6,7},{7,6},{8,9},{9,8},{10,11... | collective-permute-start | bytes 393224 | tf_op jit(solution)/shard_map/ppermute | solution.py:243
  11.2 0.9 %copy-start = (f32[2,128,128]{2,1,0:T(8,128)S(1)}, f32[2,128,128]{2,1,0:T(8,128)}, u32[]{:S(2)}) copy-start(f32[2,128,128]{2,1,0:T(8,128)} %project.1.low_ref) | copy-start | bytes 393220

commit v3 on v2

--- a/solution.py
+++ b/solution.py
@@ -12,6 +12,7 @@
 LANES = 128
 NT = (((1,), (1,)), ((), ()))
 TN = (((0,), (0,)), ((), ()))
+PIECE = 4096
 VMEM_BYTES = 60 * 2**20
 SMALL_BYTES = 8 * 2**20
 
@@ -21,8 +22,7 @@
     for which in sorted(range(len(widths)), key=lambda i: -widths[i]):
         start = 0
         while start < widths[which]:
-            left = widths[which] - start
-            size = left if left <= 6144 else 4096
+            size = (widths[which] - start) % PIECE or PIECE
             plan.append((which, start, size))
             start += size
     return plan
@@ -36,23 +36,18 @@
 def project_kernel(plan, halves, *refs):
     x_hbm, w_hbm, outs = refs[0:4], refs[4:8], refs[8:9]
     x_vmem, w_vmem, x_sem, w_sem = refs[9:13], refs[13:17], refs[17], refs[18]
-    w_copies = [pltpu.make_async_copy(w_hbm[i], w_vmem[i], w_sem.at[i]) for i in range(4)]
-    x_copies = [
-        pltpu.make_async_copy(
-            x_hbm[i].at[:, pl.ds(start, size)], x_vmem[i].at[:, pl.ds(start, size)], x_sem.at[n]
-        )
-        for n, (i, start, size) in enumerate(plan)
-    ]
+    w_copies, x_copies = [], []
     for n, (i, start, size) in enumerate(plan):
-        if start == 0:
-            w_copies[i].start()
+        piece = (slice(None), pl.ds(start, size))
+        w_copies.append(pltpu.make_async_copy(w_hbm[i].at[piece], w_vmem[i].at[piece], w_sem.at[n]))
+        x_copies.append(pltpu.make_async_copy(x_hbm[i].at[piece], x_vmem[i].at[piece], x_sem.at[n]))
+        w_copies[n].start()
         x_copies[n].start()
     tokens, rank = x_vmem[0].shape[0], w_vmem[0].shape[0]
     part = tokens // halves
     totals = {}
     for n, (i, start, size) in enumerate(plan):
-        if start == 0:
-            w_copies[i].wait()
+        w_copies[n].wait()
         x_copies[n].wait()
         w = w_vmem[i][:, pl.ds(start, size)]
         for h in range(halves):
@@ -78,7 +73,7 @@
         out_specs=(pl.BlockSpec(memory_space=pltpu.VMEM),),
         scratch_shapes=[pltpu.VMEM(x.shape, x.dtype) for x in xs]
         + [pltpu.VMEM(w.shape, w.dtype) for w in ws]
-        + [pltpu.SemaphoreType.DMA((len(plan),)), pltpu.SemaphoreType.DMA((4,))],
+        + [pltpu.SemaphoreType.DMA((len(plan),))] * 2,
         compiler_params=pltpu.CompilerParams(vmem_limit_bytes=VMEM_BYTES),
         name="project",
     )(*xs, *ws)
@@ -100,7 +95,9 @@
 
 
 def vectors_kernel(n_parts, own_rows, *refs):
-    parts, seg_ref, owner_ref, vec_ref, send_ref, slabs = refs[:n_parts], *refs[n_parts:]
+    parts, seg_ref, owner_in, vec_ref, send_ref, slabs, owner_ref, sem = refs[:n_parts], *refs[n_parts:]
+    owner_copy = pltpu.make_async_copy(owner_in, owner_ref, sem)
+    owner_copy.start()
     halves, rank = parts[0].shape[0], parts[0].shape[1] // 4
     fold = LANES // rank
     n_slabs = rank // fold
@@ -137,6 +134,7 @@
     for p in range(2):
         for k in range(col_slabs):
             vec_ref[p, :, pl.ds(k * LANES, LANES)] = slabs[p * n_slabs + t * col_slabs + k]
+    owner_copy.wait()
     for j in range(send_ref.shape[0]):
         first_row = owner_ref[j] * own_rows
         p = first_row // (rank * rank)
@@ -147,22 +145,27 @@
 
 def vectors(parts, segments, owner_map, col_width, own_rows, dp_count):
     n_slabs = (parts[0].shape[1] // 4) ** 2 // LANES
-    vmem, smem = pl.BlockSpec(memory_space=pltpu.VMEM), pl.BlockSpec(memory_space=pltpu.SMEM)
+    vmem = pl.BlockSpec(memory_space=pltpu.VMEM)
     return pl.pallas_call(
         functools.partial(vectors_kernel, len(parts), own_rows),
         out_shape=(
             jax.ShapeDtypeStruct((2, EX_DEV, col_width), jnp.float32),
             jax.ShapeDtypeStruct((dp_count, 1 + col_width // LANES, EX_DEV, LANES), jnp.float32),
         ),
-        in_specs=[vmem] * len(parts) + [vmem, smem],
+        in_specs=[vmem] * len(parts) + [vmem, pl.BlockSpec(memory_space=pl.ANY)],
         out_specs=(vmem, vmem),
-        scratch_shapes=[pltpu.VMEM((2 * n_slabs, EX_DEV, LANES), jnp.float32)],
+        scratch_shapes=[
+            pltpu.VMEM((2 * n_slabs, EX_DEV, LANES), jnp.float32),
+            pltpu.SMEM(owner_map.shape, owner_map.dtype),
+            pltpu.SemaphoreType.DMA,
+        ],
         compiler_params=pltpu.CompilerParams(vmem_limit_bytes=SMALL_BYTES),
         name="vectors",
     )(*parts, segments, owner_map)
 
 
-def fisher_kernel(scale, recv_ref, vec_ref, owner_ref, out_ref, vec_out, stack, full, sems):
+def fisher_kernel(scale, recv_ref, vec_ref, *refs):
+    out_ref, vec_out, stack, full, sems = refs[-5:]
     store = pltpu.make_async_copy(vec_ref, vec_out, sems.at[0])
     store.start()
     count, slabs = recv_ref.shape[0], recv_ref.shape[1]
@@ -172,7 +175,7 @@
     own_rows, col_width = out_ref.shape[1:]
     start = 0
     if own_rows < LANES:
-        start = (owner_ref[lax.axis_index("dp")] * own_rows) % LANES
+        start = (refs[0][lax.axis_index("dp")] * own_rows) % LANES
         start = pl.multiple_of(start, own_rows)
     row_high, row_low = split(stack[:, pl.ds(0, LANES)])
     row_wide = jnp.concatenate([row_high, row_high, row_low], axis=0)
@@ -200,13 +203,15 @@
     count, slabs = recv.shape[:2]
     col_width = (slabs - 1) * LANES
     hbm = pl.BlockSpec(memory_space=pl.ANY)
+    owners = (owner_map,) if own_rows < LANES else ()
     return pl.pallas_call(
         functools.partial(fisher_kernel, 1.0 / (EX_DEV * count)),
         out_shape=(
             jax.ShapeDtypeStruct((1, own_rows, col_width), jnp.float32),
             jax.ShapeDtypeStruct(vec.shape, vec.dtype),
         ),
-        in_specs=[pl.BlockSpec(memory_space=pltpu.VMEM), hbm, pl.BlockSpec(memory_space=pltpu.SMEM)],
+        in_specs=[pl.BlockSpec(memory_space=pltpu.VMEM), hbm]
+        + [pl.BlockSpec(memory_space=pltpu.SMEM)] * len(owners),
         out_specs=(hbm, hbm),
         scratch_shapes=[
             pltpu.VMEM((EX_DEV * count, slabs * LANES), jnp.float32),
@@ -215,7 +220,7 @@
         ],
         compiler_params=pltpu.CompilerParams(vmem_limit_bytes=SMALL_BYTES),
         name="fisher",
-    )(recv, vec, owner_map)
+    )(recv, vec, *owners)
 
 
 def shards(

time: 31.9 us -> 30.7 us (0.962)
  Pallas kernels: 9.93 us -> 8.71 us
    pallas_call x1, Pallas kernels: 1.49 us -> 0.95 us  [fisher(): pl.pallas_call(functools.partial(fisher_kernel, 1.0 / (EX_DEV * count)),...]
    pallas_call x1, Pallas kernels: 7.52 us -> 7.06 us  [project(): pl.pallas_call(functools.partial(project_kernel, plan, halves), out_shape...]
where the time goes in v3:
time: 30.7 us; the launch traced here: 30.5 us
  blocking collectives  14.4 us (47%)
  Pallas kernels  8.71 us (28%)
  starting transfers between devices  3.03 us (10%)
  waiting for transfers between devices  2.76 us (9%)
  local copies, waits for them, and re-layouts  0.95 us (3%)
  between operations  0.67 us (2%)
    all_to_all x1, blocking collectives, shards(): recv = lax.all_to_all(send, 'dp', 0, 0, tiled=True)  14.4 us
    pallas_call x1, Pallas kernels, project(): pl.pallas_call(functools.partial(project_kernel, plan, halves), out_shape...  7.06 us
    ppermute x1, starting transfers between devices, shards(): parts = (stage(own), lax.ppermute(own, 'tensor', [(0, 1), (1, 0)]))  3.03 us
    ppermute x1, waiting for transfers between devices, shards(): parts = (stage(own), lax.ppermute(own, 'tensor', [(0, 1), (1, 0)]))  2.76 us
    pallas_call x1, Pallas kernels, fisher(): pl.pallas_call(functools.partial(fisher_kernel, 1.0 / (EX_DEV * count)),...  0.95 us
    unnamed x6, local copies, waits for them, and re-layouts  0.95 us
    pallas_call x1, Pallas kernels, vectors(): pl.pallas_call(functools.partial(vectors_kernel, len(parts), own_rows), o...  0.7 us
  transfers between devices with their start and end apart: 1, of which 1 were waited for; matrix products, arithmetic and copies ran while one was open for 0% of the time, Pallas kernels for 0%

profile of v3, /device:TPU:0, one launch (start us, length us, event | category | flops | bytes accessed | tf_op | source)
XLA Modules:
  0.0 30.5 jit_solution(12385711330969078820)
XLA Ops:
  0.6 0.0 copy-start.1
  0.6 0.0 copy-start.2
  0.7 7.1 %project.1.low_ref = f32[2,128,128]{2,1,0:T(8,128)} custom-call(bf16[256,4096]{1,0:T(8,128)(2,1)} %refs_0_.1, bf16[256,4096]{1,0:T(8,128)(2,1)} %refs_1_.1, bf16[256,4096]{1,0:T(8,128)(2,1)} %refs_2_.2, bf16[256,14336]{1,0:T(8,128)(2,1)} %refs_3_.2, bf16[32,4096]{1,0:T(8,128)(2,1)} %bitcast.5, bf16[32,4096]{1,0:T(8,128)(2,1)} %bitcast.6, ...), custom_call_target="tpu_custom_call" | custom-call | tf_op jit(solution)/shard_map/project/pallas_call | solution.py:69
  7.7 3.0 %collective-permute-start = (f32[2,128,128]{2,1,0:T(8,128)}, f32[2,128,128]{2,1,0:T(8,128)S(1)}, u32[]{:S(2)}, u32[]{:S(2)}) collective-permute-start(f32[2,128,128]{2,1,0:T(8,128)} %project.1.low_ref), channel_id=1, source_target_pairs={{0,1},{1,0},{2,3},{3,2},{4,5},{5,4},{6,7},{7,6},{8,9},{9,8},{10,11... | collective-permute-start | bytes 393224 | tf_op jit(solution)/shard_map/ppermute | solution.py:248
  10.8 0.0 copy-start
  10.8 0.9 %copy-done = f32[2,128,128]{2,1,0:T(8,128)S(1)} copy-done((f32[2,128,128]{2,1,0:T(8,128)S(1)}, f32[2,128,128]{2,1,0:T(8,128)}, u32[]{:S(2)}) %copy-start) | copy-done | bytes 131096
  11.7 2.8 %collective-permute-done.refs_1_ = f32[2,128,128]{2,1,0:T(8,128)S(1)} collective-permute-done((f32[2,128,128]{2,1,0:T(8,128)}, f32[2,128,128]{2,1,0:T(8,128)S(1)}, u32[]{:S(2)}, u32[]{:S(2)}) %collective-permute-start) | collective-permute-done | bytes 131104 | tf_op jit(solution)/shard_map/ppermute | solution.py:248
  14.5 0.0 copy-done.1
  14.5 0.0 copy-done.2
  14.5 0.7 %vectors.1 = (f32[2,4,512]{2,1,0:T(4,128)S(1)}, f32[16,5,4,128]{3,2,1,0:T(4,128)S(1)}) custom-call(f32[2,128,128]{2,1,0:T(8,128)S(1)} %stage.1.refs_0_, f32[2,128,128]{2,1,0:T(8,128)S(1)} %collective-permute-done.refs_1_, s32[1,256]{1,0:T(1,128)S(1)} %copy-done.1, s32[16]{0:T(128)S(1)} %copy-done.2), custom_call_target="tpu_custom_call" | custom-call | tf_op jit(solution)/shard_map/vectors/pallas_call | solution.py:149
  15.2 14.4 %all_to_all.5.recv_ref = f32[16,5,4,128]{3,2,1,0:T(4,128)S(1)} all-to-all(f32[16,5,4,128]{3,2,1,0:T(4,128)S(1)} %get-tuple-element.6), channel_id=1, replica_groups=mesh['dp'=16,'tensor'=2] {'dp'}, dimensions={0} | all-to-all | bytes 327680 | tf_op jit(solution)/shard_map/all_to_all | solution.py:252
  29.6 1.0 %fisher.1 = (f32[1,128,512]{2,1,0:T(8,128)}, f32[2,4,512]{2,1,0:T(4,128)}) custom-call(f32[16,5,4,128]{3,2,1,0:T(4,128)S(1)} %all_to_all.5.recv_ref, f32[2,4,512]{2,1,0:T(4,128)S(1)} %get-tuple-element.7.vec_ref), custom_call_target="tpu_custom_call" | custom-call | tf_op jit(solution)/shard_map/fisher/pallas_call | solution.py:207
  (1 shorter events, 0.0 us)
Async XLA Ops:
  0.6 13.8 %copy-start.1 = (s32[1,256]{1,0:T(1,128)S(1)}, s32[1,256]{1,0:T(1,128)}, u32[]{:S(2)}) copy-start(s32[1,256]{1,0:T(1,128)} %refs_2_.3) | copy-start | bytes 3076
  0.6 13.8 %copy-start.2 = (s32[16]{0:T(128)S(1)}, s32[16]{0:T(128)}, u32[]{:S(2)}) copy-start(s32[16]{0:T(128)} %refs_3_.3) | copy-start | bytes 196
  7.7 6.7 %collective-permute-start = (f32[2,128,128]{2,1,0:T(8,128)}, f32[2,128,128]{2,1,0:T(8,128)S(1)}, u32[]{:S(2)}, u32[]{:S(2)}) collective-permute-start(f32[2,128,128]{2,1,0:T(8,128)} %project.1.low_ref), channel_id=1, source_target_pairs={{0,1},{1,0},{2,3},{3,2},{4,5},{5,4},{6,7},{7,6},{8,9},{9,8},{10,11... | collective-permute-start | bytes 393224 | tf_op jit(solution)/shard_map/ppermute | solution.py:248
  10.8 0.9 %copy-start = (f32[2,128,128]{2,1,0:T(8,128)S(1)}, f32[2,128,128]{2,1,0:T(8,128)}, u32[]{:S(2)}) copy-start(f32[2,128,128]{2,1,0:T(8,128)} %project.1.low_ref) | copy-start | bytes 393220

commit v4 on v3

--- a/solution.py
+++ b/solution.py
@@ -13,7 +13,7 @@
 NT = (((1,), (1,)), ((), ()))
 TN = (((0,), (0,)), ((), ()))
 PIECE = 4096
-VMEM_BYTES = 60 * 2**20
+VMEM_BYTES = 54976 * 2**10
 SMALL_BYTES = 8 * 2**20
 
 

time: 30.7 us -> 29.8 us (0.971)
  local copies, waits for them, and re-layouts: 0.95 us -> 0.01 us
  waiting for transfers between devices: 2.76 us -> 3.49 us
  Pallas kernels: 8.71 us -> 8.06 us
    unnamed x6 -> x4, local copies, waits for them, and re-layouts: 0.95 us -> 0.01 us
    ppermute x1, waiting for transfers between devices: 2.76 us -> 3.49 us  [shards(): parts = (stage(own), lax.ppermute(own, 'tensor', [(0, 1), (1, 0)]))]
    pallas_call x1, Pallas kernels: 7.06 us -> 6.4 us  [project(): pl.pallas_call(functools.partial(project_kernel, plan, halves), out_shape...]
where the time goes in v4:
time: 29.8 us; the launch traced here: 29.6 us
  blocking collectives  14.4 us (48%)
  Pallas kernels  8.06 us (27%)
  waiting for transfers between devices  3.49 us (12%)
  starting transfers between devices  3.03 us (10%)
  between operations  0.67 us (2%)
    all_to_all x1, blocking collectives, shards(): recv = lax.all_to_all(send, 'dp', 0, 0, tiled=True)  14.4 us
    pallas_call x1, Pallas kernels, project(): pl.pallas_call(functools.partial(project_kernel, plan, halves), out_shape...  6.4 us
    ppermute x1, waiting for transfers between devices, shards(): parts = (stage(own), lax.ppermute(own, 'tensor', [(0, 1), (1, 0)]))  3.49 us
    ppermute x1, starting transfers between devices, shards(): parts = (stage(own), lax.ppermute(own, 'tensor', [(0, 1), (1, 0)]))  3.03 us
    pallas_call x1, Pallas kernels, fisher(): pl.pallas_call(functools.partial(fisher_kernel, 1.0 / (EX_DEV * count)),...  0.95 us
    pallas_call x1, Pallas kernels, vectors(): pl.pallas_call(functools.partial(vectors_kernel, len(parts), own_rows), o...  0.7 us
  transfers between devices with their start and end apart: 1, of which 1 were waited for; matrix products, arithmetic and copies ran while one was open for 0% of the time, Pallas kernels for 0%

profile of v4, /device:TPU:0, one launch (start us, length us, event | category | flops | bytes accessed | tf_op | source)
XLA Modules:
  0.0 29.6 jit_solution(2287577282289824319)
XLA Ops:
  0.6 0.0 copy-start
  0.6 0.0 copy-start.1
  0.7 6.4 %project.1.low_ref = f32[2,128,128]{2,1,0:T(8,128)S(1)} custom-call(bf16[256,4096]{1,0:T(8,128)(2,1)} %refs_0_.1, bf16[256,4096]{1,0:T(8,128)(2,1)} %refs_1_.1, bf16[256,4096]{1,0:T(8,128)(2,1)} %refs_2_.2, bf16[256,14336]{1,0:T(8,128)(2,1)} %refs_3_.2, bf16[32,4096]{1,0:T(8,128)(2,1)} %bitcast.5, bf16[32,4096]{1,0:T(8,128)(2,1)} %bitcast.6, ...), custom_call_target="tpu_custom_call" | custom-call | tf_op jit(solution)/shard_map/project/pallas_call | solution.py:69
  7.1 3.0 %collective-permute-start = (f32[2,128,128]{2,1,0:T(8,128)S(1)}, f32[2,128,128]{2,1,0:T(8,128)S(1)}, u32[]{:S(2)}, u32[]{:S(2)}) collective-permute-start(f32[2,128,128]{2,1,0:T(8,128)S(1)} %project.1.low_ref), channel_id=1, source_target_pairs={{0,1},{1,0},{2,3},{3,2},{4,5},{5,4},{6,7},{7,6},{8,9},{9,8},{10,11... | collective-permute-start | bytes 393224 | tf_op jit(solution)/shard_map/ppermute | solution.py:248
  10.1 3.5 %collective-permute-done.refs_1_ = f32[2,128,128]{2,1,0:T(8,128)S(1)} collective-permute-done((f32[2,128,128]{2,1,0:T(8,128)S(1)}, f32[2,128,128]{2,1,0:T(8,128)S(1)}, u32[]{:S(2)}, u32[]{:S(2)}) %collective-permute-start) | collective-permute-done | bytes 131104 | tf_op jit(solution)/shard_map/ppermute | solution.py:248
  13.6 0.0 copy-done
  13.6 0.0 copy-done.1
  13.6 0.7 %vectors.1 = (f32[2,4,512]{2,1,0:T(4,128)S(1)}, f32[16,5,4,128]{3,2,1,0:T(4,128)S(1)}) custom-call(f32[2,128,128]{2,1,0:T(8,128)S(1)} %stage.1.refs_0_, f32[2,128,128]{2,1,0:T(8,128)S(1)} %collective-permute-done.refs_1_, s32[1,256]{1,0:T(1,128)S(1)} %copy-done, s32[16]{0:T(128)S(1)} %copy-done.1), custom_call_target="tpu_custom_call" | custom-call | tf_op jit(solution)/shard_map/vectors/pallas_call | solution.py:149
  14.3 14.4 %all_to_all.5.recv_ref = f32[16,5,4,128]{3,2,1,0:T(4,128)S(1)} all-to-all(f32[16,5,4,128]{3,2,1,0:T(4,128)S(1)} %get-tuple-element.6), channel_id=1, replica_groups=mesh['dp'=16,'tensor'=2] {'dp'}, dimensions={0} | all-to-all | bytes 327680 | tf_op jit(solution)/shard_map/all_to_all | solution.py:252
  28.7 0.9 %fisher.1 = (f32[1,128,512]{2,1,0:T(8,128)}, f32[2,4,512]{2,1,0:T(4,128)}) custom-call(f32[16,5,4,128]{3,2,1,0:T(4,128)S(1)} %all_to_all.5.recv_ref, f32[2,4,512]{2,1,0:T(4,128)S(1)} %get-tuple-element.7.vec_ref), custom_call_target="tpu_custom_call" | custom-call | tf_op jit(solution)/shard_map/fisher/pallas_call | solution.py:207
  (1 shorter events, 0.0 us)
Async XLA Ops:
  0.6 13.0 %copy-start = (s32[1,256]{1,0:T(1,128)S(1)}, s32[1,256]{1,0:T(1,128)}, u32[]{:S(2)}) copy-start(s32[1,256]{1,0:T(1,128)} %refs_2_.3) | copy-start | bytes 3076
  0.6 13.0 %copy-start.1 = (s32[16]{0:T(128)S(1)}, s32[16]{0:T(128)}, u32[]{:S(2)}) copy-start(s32[16]{0:T(128)} %refs_3_.3) | copy-start | bytes 196
  7.1 6.5 %collective-permute-start = (f32[2,128,128]{2,1,0:T(8,128)S(1)}, f32[2,128,128]{2,1,0:T(8,128)S(1)}, u32[]{:S(2)}, u32[]{:S(2)}) collective-permute-start(f32[2,128,128]{2,1,0:T(8,128)S(1)} %project.1.low_ref), channel_id=1, source_target_pairs={{0,1},{1,0},{2,3},{3,2},{4,5},{5,4},{6,7},{7,6},{8,9},{9,8},{10,11... | collective-permute-start | bytes 393224 | tf_op jit(solution)/shard_map/ppermute | solution.py:248

commit v5 on v4

--- a/solution.py
+++ b/solution.py
@@ -94,10 +94,8 @@
     )(low)
 
 
-def vectors_kernel(n_parts, own_rows, *refs):
-    parts, seg_ref, owner_in, vec_ref, send_ref, slabs, owner_ref, sem = refs[:n_parts], *refs[n_parts:]
-    owner_copy = pltpu.make_async_copy(owner_in, owner_ref, sem)
-    owner_copy.start()
+def vectors_kernel(n_parts, *refs):
+    parts, seg_ref, wanted_ref, vec_ref, send_ref, slabs = refs[:n_parts], *refs[n_parts:]
     halves, rank = parts[0].shape[0], parts[0].shape[1] // 4
     fold = LANES // rank
     n_slabs = rank // fold
@@ -131,37 +129,36 @@
                 [flat[e * n_slabs + g : e * n_slabs + g + 1] for e in range(EX_DEV)], axis=0
             )
     t = lax.axis_index("tensor")
+    columns = [[slabs[p * n_slabs + t * col_slabs + k] for k in range(col_slabs)] for p in range(2)]
     for p in range(2):
         for k in range(col_slabs):
-            vec_ref[p, :, pl.ds(k * LANES, LANES)] = slabs[p * n_slabs + t * col_slabs + k]
-    owner_copy.wait()
+            vec_ref[p, :, pl.ds(k * LANES, LANES)] = columns[p][k]
+    rows = [slabs[s] for s in range(2 * n_slabs)]
     for j in range(send_ref.shape[0]):
-        first_row = owner_ref[j] * own_rows
-        p = first_row // (rank * rank)
-        send_ref[j, 0] = slabs[first_row // LANES]
+        wanted = wanted_ref[j]
+        row_slab = rows[0]
+        for s in range(1, 2 * n_slabs):
+            row_slab = jnp.where(wanted == s, rows[s], row_slab)
+        send_ref[j, 0] = row_slab
         for k in range(col_slabs):
-            send_ref[j, 1 + k] = slabs[p * n_slabs + t * col_slabs + k]
-
-
-def vectors(parts, segments, owner_map, col_width, own_rows, dp_count):
+            send_ref[j, 1 + k] = jnp.where(wanted < n_slabs, columns[0][k], columns[1][k])
+
+
+def vectors(parts, segments, wanted, col_width):
     n_slabs = (parts[0].shape[1] // 4) ** 2 // LANES
     vmem = pl.BlockSpec(memory_space=pltpu.VMEM)
     return pl.pallas_call(
-        functools.partial(vectors_kernel, len(parts), own_rows),
+        functools.partial(vectors_kernel, len(parts)),
         out_shape=(
             jax.ShapeDtypeStruct((2, EX_DEV, col_width), jnp.float32),
-            jax.ShapeDtypeStruct((dp_count, 1 + col_width // LANES, EX_DEV, LANES), jnp.float32),
+            jax.ShapeDtypeStruct((wanted.shape[0], 1 + col_width // LANES, EX_DEV, LANES), jnp.float32),
         ),
-        in_specs=[vmem] * len(parts) + [vmem, pl.BlockSpec(memory_space=pl.ANY)],
+        in_specs=[vmem] * (len(parts) + 2),
         out_specs=(vmem, vmem),
-        scratch_shapes=[
-            pltpu.VMEM((2 * n_slabs, EX_DEV, LANES), jnp.float32),
-            pltpu.SMEM(owner_map.shape, owner_map.dtype),
-            pltpu.SemaphoreType.DMA,
-        ],
+        scratch_shapes=[pltpu.VMEM((2 * n_slabs, EX_DEV, LANES), jnp.float32)],
         compiler_params=pltpu.CompilerParams(vmem_limit_bytes=SMALL_BYTES),
         name="vectors",
-    )(*parts, segments, owner_map)
+    )(*parts, segments, wanted)
 
 
 def fisher_kernel(scale, recv_ref, vec_ref, *refs):
@@ -248,7 +245,8 @@
         parts = (stage(own), lax.ppermute(own, "tensor", [(0, 1), (1, 0)]))
     else:
         parts = (lax.psum(own, "tensor"),)
-    vec, send = vectors(parts, segment_ids, owner_map, col_width, own_rows, dp_count)
+    wanted = jnp.broadcast_to((owner_map * own_rows // LANES)[:, None, None], (dp_count, EX_DEV, LANES))
+    vec, send = vectors(parts, segment_ids, wanted, col_width)
     recv = lax.all_to_all(send, "dp", 0, 0, tiled=True)
     fisher_block, example_vectors = fisher(recv, vec, owner_map, own_rows)
     return example_vectors, fisher_block

time: 29.8 us -> 29.6 us (level)
  Pallas kernels: 8.06 us -> 7.72 us
    pallas_call x1, Pallas kernels: 0.7 us -> 0.36 us  [vectors(): pl.pallas_call(functools.partial(vectors_kernel, len(parts)), out_shape=(...]
where the time goes in v5:
time: 29.6 us; the launch traced here: 29.4 us
  blocking collectives  14.4 us (49%)
  Pallas kernels  7.72 us (26%)
  waiting for transfers between devices  3.46 us (12%)
  starting transfers between devices  3.03 us (10%)
  between operations  0.69 us (2%)
    all_to_all x1, blocking collectives, shards(): recv = lax.all_to_all(send, 'dp', 0, 0, tiled=True)  14.4 us
    pallas_call x1, Pallas kernels, project(): pl.pallas_call(functools.partial(project_kernel, plan, halves), out_shape...  6.4 us
    ppermute x1, waiting for transfers between devices, shards(): parts = (stage(own), lax.ppermute(own, 'tensor', [(0, 1), (1, 0)]))  3.46 us
    ppermute x1, starting transfers between devices, shards(): parts = (stage(own), lax.ppermute(own, 'tensor', [(0, 1), (1, 0)]))  3.03 us
    pallas_call x1, Pallas kernels, fisher(): pl.pallas_call(functools.partial(fisher_kernel, 1.0 / (EX_DEV * count)),...  0.95 us
  transfers between devices with their start and end apart: 1, of which 1 were waited for; matrix products, arithmetic and copies ran while one was open for 0% of the time, Pallas kernels for 0%

profile of v5, /device:TPU:0, one launch (start us, length us, event | category | flops | bytes accessed | tf_op | source)
XLA Modules:
  0.0 29.4 jit_solution(18342911663224941140)
XLA Ops:
  0.6 0.0 copy-start.1
  0.6 0.0 copy-start
  0.7 6.4 %project.1.low_ref = f32[2,128,128]{2,1,0:T(8,128)S(1)} custom-call(bf16[256,4096]{1,0:T(8,128)(2,1)} %refs_0_.1, bf16[256,4096]{1,0:T(8,128)(2,1)} %refs_1_.1, bf16[256,4096]{1,0:T(8,128)(2,1)} %refs_2_.2, bf16[256,14336]{1,0:T(8,128)(2,1)} %refs_3_.1, bf16[32,4096]{1,0:T(8,128)(2,1)} %bitcast.5, bf16[32,4096]{1,0:T(8,128)(2,1)} %bitcast.6, ...), custom_call_target="tpu_custom_call" | custom-call | tf_op jit(solution)/shard_map/project/pallas_call | solution.py:69
  7.1 3.0 %collective-permute-start = (f32[2,128,128]{2,1,0:T(8,128)S(1)}, f32[2,128,128]{2,1,0:T(8,128)S(1)}, u32[]{:S(2)}, u32[]{:S(2)}) collective-permute-start(f32[2,128,128]{2,1,0:T(8,128)S(1)} %project.1.low_ref), channel_id=1, source_target_pairs={{0,1},{1,0},{2,3},{3,2},{4,5},{5,4},{6,7},{7,6},{8,9},{9,8},{10,11... | collective-permute-start | bytes 393224 | tf_op jit(solution)/shard_map/ppermute | solution.py:245
  10.1 0.0 copy-done.1
  10.1 3.5 %collective-permute-done.refs_1_ = f32[2,128,128]{2,1,0:T(8,128)S(1)} collective-permute-done((f32[2,128,128]{2,1,0:T(8,128)S(1)}, f32[2,128,128]{2,1,0:T(8,128)S(1)}, u32[]{:S(2)}, u32[]{:S(2)}) %collective-permute-start) | collective-permute-done | bytes 131104 | tf_op jit(solution)/shard_map/ppermute | solution.py:245
  13.6 0.1 broadcast_in_dim.2.refs_3_
  13.7 0.0 copy-done
  13.7 0.4 %vectors.1 = (f32[2,4,512]{2,1,0:T(4,128)S(1)}, f32[16,5,4,128]{3,2,1,0:T(4,128)S(1)}) custom-call(f32[2,128,128]{2,1,0:T(8,128)S(1)} %stage.1.refs_0_, f32[2,128,128]{2,1,0:T(8,128)S(1)} %collective-permute-done.refs_1_, s32[1,256]{1,0:T(1,128)S(1)} %copy-done, s32[16,4,128]{2,1,0:T(4,128)S(1)} %broadcast_in_dim.2.refs_3_), custom_call_target="tpu_custom_call" | custom-call | tf_op jit(solution)/shard_map/vectors/pallas_call | solution.py:150
  14.1 14.4 %all_to_all.5.recv_ref = f32[16,5,4,128]{3,2,1,0:T(4,128)S(1)} all-to-all(f32[16,5,4,128]{3,2,1,0:T(4,128)S(1)} %get-tuple-element.6), channel_id=1, replica_groups=mesh['dp'=16,'tensor'=2] {'dp'}, dimensions={0} | all-to-all | bytes 327680 | tf_op jit(solution)/shard_map/all_to_all | solution.py:250
  28.4 0.9 %fisher.1 = (f32[1,128,512]{2,1,0:T(8,128)}, f32[2,4,512]{2,1,0:T(4,128)}) custom-call(f32[16,5,4,128]{3,2,1,0:T(4,128)S(1)} %all_to_all.5.recv_ref, f32[2,4,512]{2,1,0:T(4,128)S(1)} %get-tuple-element.7.vec_ref), custom_call_target="tpu_custom_call" | custom-call | tf_op jit(solution)/shard_map/fisher/pallas_call | solution.py:204
  (2 shorter events, 0.0 us)
Async XLA Ops:
  0.6 9.5 %copy-start.1 = (s32[16]{0:T(128)S(1)}, s32[16]{0:T(128)}, u32[]{:S(2)}) copy-start(s32[16]{0:T(128)} %param.19) | copy-start | bytes 196
  0.6 13.0 %copy-start = (s32[1,256]{1,0:T(1,128)S(1)}, s32[1,256]{1,0:T(1,128)}, u32[]{:S(2)}) copy-start(s32[1,256]{1,0:T(1,128)} %refs_2_.3) | copy-start | bytes 3076
  7.1 6.5 %collective-permute-start = (f32[2,128,128]{2,1,0:T(8,128)S(1)}, f32[2,128,128]{2,1,0:T(8,128)S(1)}, u32[]{:S(2)}, u32[]{:S(2)}) collective-permute-start(f32[2,128,128]{2,1,0:T(8,128)S(1)} %project.1.low_ref), channel_id=1, source_target_pairs={{0,1},{1,0},{2,3},{3,2},{4,5},{5,4},{6,7},{7,6},{8,9},{9,8},{10,11... | collective-permute-start | bytes 393224 | tf_op jit(solution)/shard_map/ppermute | solution.py:245

commit v6 on v5

--- a/solution.py
+++ b/solution.py
@@ -13,6 +13,9 @@
 NT = (((1,), (1,)), ((), ()))
 TN = (((0,), (0,)), ((), ()))
 PIECE = 4096
+PLANE = 4
+PLANE_SHIFTS = (2, 1, 3)
+PLANE_STEPS = (2, 3, 1)
 VMEM_BYTES = 54976 * 2**10
 SMALL_BYTES = 8 * 2**20
 
@@ -94,8 +97,9 @@
     )(low)
 
 
-def vectors_kernel(n_parts, *refs):
-    parts, seg_ref, wanted_ref, vec_ref, send_ref, slabs = refs[:n_parts], *refs[n_parts:]
+def vectors_kernel(n_parts, n_sends, *refs):
+    parts, seg_ref, wanted_ref, vec_ref = refs[:n_parts], *refs[n_parts : n_parts + 3]
+    send_refs, slabs = refs[n_parts + 3 : n_parts + 3 + n_sends], refs[n_parts + 3 + n_sends]
     halves, rank = parts[0].shape[0], parts[0].shape[1] // 4
     fold = LANES // rank
     n_slabs = rank // fold
@@ -134,45 +138,88 @@
         for k in range(col_slabs):
             vec_ref[p, :, pl.ds(k * LANES, LANES)] = columns[p][k]
     rows = [slabs[s] for s in range(2 * n_slabs)]
-    for j in range(send_ref.shape[0]):
+    for j in range(wanted_ref.shape[0]):
         wanted = wanted_ref[j]
         row_slab = rows[0]
         for s in range(1, 2 * n_slabs):
             row_slab = jnp.where(wanted == s, rows[s], row_slab)
-        send_ref[j, 0] = row_slab
+        if n_sends > 1:
+            refs[-1][j] = row_slab
+            continue
+        send_refs[0][j, 0] = row_slab
         for k in range(col_slabs):
-            send_ref[j, 1 + k] = jnp.where(wanted < n_slabs, columns[0][k], columns[1][k])
-
-
-def vectors(parts, segments, wanted, col_width):
+            send_refs[0][j, 1 + k] = jnp.where(wanted < n_slabs, columns[0][k], columns[1][k])
+    if n_sends > 1:
+        plane = lax.axis_index("dp") // PLANE
+        for shift, send_ref in enumerate(send_refs):
+            for p in range(2):
+                for k in range(col_slabs):
+                    send_ref[p * col_slabs + k] = columns[p][k]
+            for d in range(PLANE):
+                send_ref[2 * col_slabs + d] = refs[-1][lax.rem(plane + shift, n_sends) * PLANE + d]
+
+
+def vectors(parts, segments, wanted, col_width, sends):
     n_slabs = (parts[0].shape[1] // 4) ** 2 // LANES
     vmem = pl.BlockSpec(memory_space=pltpu.VMEM)
     return pl.pallas_call(
-        functools.partial(vectors_kernel, len(parts)),
-        out_shape=(
-            jax.ShapeDtypeStruct((2, EX_DEV, col_width), jnp.float32),
-            jax.ShapeDtypeStruct((wanted.shape[0], 1 + col_width // LANES, EX_DEV, LANES), jnp.float32),
-        ),
+        functools.partial(vectors_kernel, len(parts), len(sends)),
+        out_shape=[jax.ShapeDtypeStruct((2, EX_DEV, col_width), jnp.float32)]
+        + [jax.ShapeDtypeStruct(shape + (EX_DEV, LANES), jnp.float32) for shape in sends],
         in_specs=[vmem] * (len(parts) + 2),
-        out_specs=(vmem, vmem),
-        scratch_shapes=[pltpu.VMEM((2 * n_slabs, EX_DEV, LANES), jnp.float32)],
+        out_specs=[vmem] * (1 + len(sends)),
+        scratch_shapes=[
+            pltpu.VMEM((2 * n_slabs, EX_DEV, LANES), jnp.float32),
+            pltpu.VMEM((wanted.shape[0], EX_DEV, LANES), jnp.float32),
+        ],
         compiler_params=pltpu.CompilerParams(vmem_limit_bytes=SMALL_BYTES),
         name="vectors",
     )(*parts, segments, wanted)
 
 
-def fisher_kernel(scale, recv_ref, vec_ref, *refs):
-    out_ref, vec_out, stack, full, sems = refs[-5:]
+def regroup_kernel(n_slabs, *refs):
+    blocks, wanted_ref, outs = refs[: len(refs) // 2], refs[len(refs) // 2], refs[len(refs) // 2 + 1 :]
+    col_slabs = (blocks[0].shape[0] - PLANE) // 2
+    me = lax.axis_index("dp")
+    plane, place = me // PLANE, lax.rem(me, PLANE)
+    for step, out in zip((0,) + PLANE_STEPS, outs):
+        target = place ^ step
+        first = wanted_ref[plane * PLANE + target] < n_slabs
+        for i, block in enumerate(blocks):
+            rows = pl.ds(i * EX_DEV, EX_DEV)
+            out[0, rows, :] = block[2 * col_slabs + target]
+            for k in range(col_slabs):
+                out[1 + k, rows, :] = jnp.where(first, block[k], block[col_slabs + k])
+
+
+def regroup(blocks, wanted, n_slabs):
+    col_slabs = (blocks[0].shape[0] - PLANE) // 2
+    vmem = pl.BlockSpec(memory_space=pltpu.VMEM)
+    part = jax.ShapeDtypeStruct((1 + col_slabs, len(blocks) * EX_DEV, LANES), jnp.float32)
+    return pl.pallas_call(
+        functools.partial(regroup_kernel, n_slabs),
+        out_shape=[part] * PLANE,
+        in_specs=[vmem] * (len(blocks) + 1),
+        out_specs=[vmem] * PLANE,
+        compiler_params=pltpu.CompilerParams(vmem_limit_bytes=SMALL_BYTES),
+        name="regroup",
+    )(*blocks, wanted)
+
+
+def fisher_kernel(scale, n_parts, *refs):
+    parts, vec_ref, (out_ref, vec_out, stack, full, sems) = refs[:n_parts], refs[n_parts], refs[-5:]
     store = pltpu.make_async_copy(vec_ref, vec_out, sems.at[0])
     store.start()
-    count, slabs = recv_ref.shape[0], recv_ref.shape[1]
-    for i in range(count):
+    examples, slabs = stack.shape[0], stack.shape[1] // LANES
+    pieces = [part.at[i] for part in parts for i in range(part.shape[0])]
+    rows = examples // len(pieces)
+    for i, piece in enumerate(pieces):
         for k in range(slabs):
-            stack[pl.ds(i * EX_DEV, EX_DEV), pl.ds(k * LANES, LANES)] = recv_ref[i, k]
+            stack[pl.ds(i * rows, rows), pl.ds(k * LANES, LANES)] = piece[k]
     own_rows, col_width = out_ref.shape[1:]
     start = 0
     if own_rows < LANES:
-        start = (refs[0][lax.axis_index("dp")] * own_rows) % LANES
+        start = (refs[n_parts + 1][lax.axis_index("dp")] * own_rows) % LANES
         start = pl.multiple_of(start, own_rows)
     row_high, row_low = split(stack[:, pl.ds(0, LANES)])
     row_wide = jnp.concatenate([row_high, row_high, row_low], axis=0)
@@ -196,28 +243,29 @@
         store.wait()
 
 
-def fisher(recv, vec, owner_map, own_rows):
-    count, slabs = recv.shape[:2]
+def fisher(parts, vec, owner_map, own_rows):
+    slabs = parts[0].shape[1]
+    examples = sum(part.shape[0] * part.shape[2] for part in parts)
     col_width = (slabs - 1) * LANES
     hbm = pl.BlockSpec(memory_space=pl.ANY)
     owners = (owner_map,) if own_rows < LANES else ()
     return pl.pallas_call(
-        functools.partial(fisher_kernel, 1.0 / (EX_DEV * count)),
+        functools.partial(fisher_kernel, 1.0 / examples, len(parts)),
         out_shape=(
             jax.ShapeDtypeStruct((1, own_rows, col_width), jnp.float32),
             jax.ShapeDtypeStruct(vec.shape, vec.dtype),
         ),
-        in_specs=[pl.BlockSpec(memory_space=pltpu.VMEM), hbm]
+        in_specs=[pl.BlockSpec(memory_space=pltpu.VMEM)] * len(parts) + [hbm]
         + [pl.BlockSpec(memory_space=pltpu.SMEM)] * len(owners),
         out_specs=(hbm, hbm),
         scratch_shapes=[
-            pltpu.VMEM((EX_DEV * count, slabs * LANES), jnp.float32),
+            pltpu.VMEM((examples, slabs * LANES), jnp.float32),
             pltpu.VMEM((LANES, col_width), jnp.float32),
             pltpu.SemaphoreType.DMA((3,)),
         ],
         compiler_params=pltpu.CompilerParams(vmem_limit_bytes=SMALL_BYTES),
         name="fisher",
-    )(recv, vec, *owners)
+    )(*parts, vec, *owners)
 
 
 def shards(
@@ -246,8 +294,22 @@
     else:
         parts = (lax.psum(own, "tensor"),)
     wanted = jnp.broadcast_to((owner_map * own_rows // LANES)[:, None, None], (dp_count, EX_DEV, LANES))
-    vec, send = vectors(parts, segment_ids, wanted, col_width)
-    recv = lax.all_to_all(send, "dp", 0, 0, tiled=True)
+    col_slabs = col_width // LANES
+    planes = dp_count // PLANE
+    if planes == 4 and own_rows == LANES:
+        block = (2 * col_slabs + PLANE,)
+        vec, *blocks = vectors(parts, segment_ids, wanted, col_width, [block] * planes)
+        for shift in PLANE_SHIFTS:
+            pairs = [(i, (i + shift * PLANE) % dp_count) for i in range(dp_count)]
+            blocks[shift] = lax.ppermute(blocks[shift], "dp", pairs)
+        grouped = regroup(blocks, wanted, width // LANES)
+        recv = [grouped[0]]
+        for part, step in zip(grouped[1:], PLANE_STEPS):
+            recv.append(lax.ppermute(part, "dp", [(i, i ^ step) for i in range(dp_count)]))
+        recv = [part[None] for part in recv]
+    else:
+        vec, send = vectors(parts, segment_ids, wanted, col_width, [(dp_count, 1 + col_slabs)])
+        recv = [lax.all_to_all(send, "dp", 0, 0, tiled=True)]
     fisher_block, example_vectors = fisher(recv, vec, owner_map, own_rows)
     return example_vectors, fisher_block
 

time: 29.6 us -> 28.4 us (0.959)
  blocking collectives: 14.4 us -> 0 us
  starting transfers between devices: 3.03 us -> 11 us
  waiting for transfers between devices: 3.46 us -> 8.7 us
    all_to_all x1 -> x0, blocking collectives: 14.4 us -> none  [shards(): recv = lax.all_to_all(send, 'dp', 0, 0, tiled=True)]
    ppermute x0 -> x6, starting transfers between devices: none -> 7.99 us  [the longest x3 5.79 us: shards(): blocks[shift] = lax.ppermute(blocks[shift], 'dp', pairs)]
    ppermute x0 -> x6, waiting for transfers between devices: none -> 5.24 us  [the longest x3 2.76 us: shards(): lax.ppermute(part, 'dp', [(i, i ^ step) for i in range(dp_count)])]
    pallas_call x2 -> x3, Pallas kernels: 1.31 us -> 1.33 us  [the longest x1 0.94 us: fisher(): pl.pallas_call(functools.partial(fisher_kernel, 1.0 / examples, len(parts...]
  transfers between devices with their start and end apart: 1 -> 7, of which waited for: 1 -> 5; matrix products, arithmetic and copies ran while one was open for 0% -> 0% of each run, Pallas kernels for 0% -> 0%
where the time goes in v6:
time: 28.4 us; the launch traced here: 28.3 us
  starting transfers between devices  11 us (39%)
  waiting for transfers between devices  8.7 us (31%)
  Pallas kernels  7.75 us (27%)
  between operations  0.7 us (2%)
    pallas_call x1, Pallas kernels, project(): pl.pallas_call(functools.partial(project_kernel, plan, halves), out_shape...  6.4 us
    ppermute x3, starting transfers between devices, shards(): blocks[shift] = lax.ppermute(blocks[shift], 'dp', pairs)  5.79 us
    ppermute x1, waiting for transfers between devices, shards(): parts = (stage(own), lax.ppermute(own, 'tensor', [(0, 1), (1, 0)]))  3.46 us
    ppermute x1, starting transfers between devices, shards(): parts = (stage(own), lax.ppermute(own, 'tensor', [(0, 1), (1, 0)]))  3.03 us
    ppermute x3, waiting for transfers between devices, shards(): lax.ppermute(part, 'dp', [(i, i ^ step) for i in range(dp_count)])  2.76 us
    ppermute x3, waiting for transfers between devices, shards(): blocks[shift] = lax.ppermute(blocks[shift], 'dp', pairs)  2.48 us
    ppermute x3, starting transfers between devices, shards(): lax.ppermute(part, 'dp', [(i, i ^ step) for i in range(dp_count)])  2.21 us
    pallas_call x1, Pallas kernels, fisher(): pl.pallas_call(functools.partial(fisher_kernel, 1.0 / examples, len(parts...  0.94 us
  transfers between devices with their start and end apart: 7, of which 5 were waited for; matrix products, arithmetic and copies ran while one was open for 0% of the time, Pallas kernels for 0%

profile of v6, /device:TPU:0, one launch (start us, length us, event | category | flops | bytes accessed | tf_op | source)
XLA Modules:
  0.0 28.3 jit_solution(13001862562426920748)
XLA Ops:
  0.6 0.0 copy-start.1
  0.6 0.0 copy-start
  0.7 6.4 %project.1.low_ref = f32[2,128,128]{2,1,0:T(8,128)S(1)} custom-call(bf16[256,4096]{1,0:T(8,128)(2,1)} %refs_0_.1, bf16[256,4096]{1,0:T(8,128)(2,1)} %refs_1_.1, bf16[256,4096]{1,0:T(8,128)(2,1)} %refs_2_.2, bf16[256,14336]{1,0:T(8,128)(2,1)} %refs_3_.1, bf16[32,4096]{1,0:T(8,128)(2,1)} %bitcast.13, bf16[32,4096]{1,0:T(8,128)(2,1)} %bitcast.14, ...), custom_call_target="tpu_custom_call" | custom-call | tf_op jit(solution)/shard_map/project/pallas_call | solution.py:72
  7.1 3.0 %collective-permute-start = (f32[2,128,128]{2,1,0:T(8,128)S(1)}, f32[2,128,128]{2,1,0:T(8,128)S(1)}, u32[]{:S(2)}, u32[]{:S(2)}) collective-permute-start(f32[2,128,128]{2,1,0:T(8,128)S(1)} %project.1.low_ref), channel_id=1, source_target_pairs={{0,1},{1,0},{2,3},{3,2},{4,5},{5,4},{6,7},{7,6},{8,9},{9,8},{10,11... | collective-permute-start | bytes 393224 | tf_op jit(solution)/shard_map/ppermute | solution.py:293
  10.1 0.0 copy-done.1
  10.1 3.5 %collective-permute-done.refs_1_ = f32[2,128,128]{2,1,0:T(8,128)S(1)} collective-permute-done((f32[2,128,128]{2,1,0:T(8,128)S(1)}, f32[2,128,128]{2,1,0:T(8,128)S(1)}, u32[]{:S(2)}, u32[]{:S(2)}) %collective-permute-start) | collective-permute-done | bytes 131104 | tf_op jit(solution)/shard_map/ppermute | solution.py:293
  13.6 0.1 broadcast_in_dim.18.refs_3_.refs_4_
  13.7 0.0 copy-done
  13.7 0.4 %vectors.1 = (f32[2,4,512]{2,1,0:T(4,128)S(1)}, f32[12,4,128]{2,1,0:T(4,128)S(1)}, f32[12,4,128]{2,1,0:T(4,128)S(1)}, f32[12,4,128]{2,1,0:T(4,128)S(1)}, f32[12,4,128]{2,1,0:T(4,128)S(1)}) custom-call(f32[2,128,128]{2,1,0:T(8,128)S(1)} %stage.1.refs_0_, f32[2,128,128]{2,1,0:T(8,128)S(1)} %collective-permute-done.refs_1_, s32[1,256]{1,0:T(1,128)S(1)} %copy-done, ...), custom_call_target="tpu_custom_call" | custom-call | tf_op jit(solution)/shard_map/vectors/pallas_call | solution.py:165
  14.0 1.8 %collective-permute-start.1 = (f32[12,4,128]{2,1,0:T(4,128)S(1)}, f32[12,4,128]{2,1,0:T(4,128)S(1)}, u32[]{:S(2)}, u32[]{:S(2)}) collective-permute-start(f32[12,4,128]{2,1,0:T(4,128)S(1)} %get-tuple-element.14), channel_id=1, source_target_pairs={{0,8},{2,10},{4,12},{6,14},{8,16},{10,18},{12,20},{14,22},{16,24},... | collective-permute-start | bytes 73736 | tf_op jit(solution)/shard_map/ppermute | solution.py:304
  15.9 2.6 %collective-permute-start.2 = (f32[12,4,128]{2,1,0:T(4,128)S(1)}, f32[12,4,128]{2,1,0:T(4,128)S(1)}, u32[]{:S(2)}, u32[]{:S(2)}) collective-permute-start(f32[12,4,128]{2,1,0:T(4,128)S(1)} %get-tuple-element.15), channel_id=1, source_target_pairs={{0,16},{2,18},{4,20},{6,22},{8,24},{10,26},{12,28},{14,30},{16,0},... | collective-permute-start | bytes 73736 | tf_op jit(solution)/shard_map/ppermute | solution.py:304
  18.5 1.3 %collective-permute-start.3 = (f32[12,4,128]{2,1,0:T(4,128)S(1)}, f32[12,4,128]{2,1,0:T(4,128)S(1)}, u32[]{:S(2)}, u32[]{:S(2)}) collective-permute-start(f32[12,4,128]{2,1,0:T(4,128)S(1)} %get-tuple-element.16), channel_id=1, source_target_pairs={{0,24},{2,26},{4,28},{6,30},{8,0},{10,2},{12,4},{14,6},{16,8},{18,... | collective-permute-start | bytes 73736 | tf_op jit(solution)/shard_map/ppermute | solution.py:304
  19.8 0.0 collective-permute-done.1.refs_1_
  19.9 0.7 %collective-permute-done.2.refs_2_ = f32[12,4,128]{2,1,0:T(4,128)S(1)} collective-permute-done((f32[12,4,128]{2,1,0:T(4,128)S(1)}, f32[12,4,128]{2,1,0:T(4,128)S(1)}, u32[]{:S(2)}, u32[]{:S(2)}) %collective-permute-start.2) | collective-permute-done | bytes 24608 | tf_op jit(solution)/shard_map/ppermute | solution.py:304
  20.6 1.7 %collective-permute-done.3.refs_3_ = f32[12,4,128]{2,1,0:T(4,128)S(1)} collective-permute-done((f32[12,4,128]{2,1,0:T(4,128)S(1)}, f32[12,4,128]{2,1,0:T(4,128)S(1)}, u32[]{:S(2)}, u32[]{:S(2)}) %collective-permute-start.3) | collective-permute-done | bytes 24608 | tf_op jit(solution)/shard_map/ppermute | solution.py:304
  22.4 1.5 %collective-permute-start.4 = (f32[5,16,128]{2,1,0:T(8,128)S(1)}, f32[5,16,128]{2,1,0:T(8,128)S(1)}, u32[]{:S(2)}, u32[]{:S(2)}) collective-permute-start(f32[5,16,128]{2,1,0:T(8,128)S(1)} %get-tuple-element.18), channel_id=1, source_target_pairs={{0,4},{2,6},{4,0},{6,2},{8,12},{10,14},{12,8},{14,10},{16,20},{18,... | collective-permute-start | bytes 122888 | tf_op jit(solution)/shard_map/ppermute | solution.py:308
  23.9 0.0 collective-permute-start.5
  23.9 0.7 %collective-permute-start.6 = (f32[5,16,128]{2,1,0:T(8,128)S(1)}, f32[5,16,128]{2,1,0:T(8,128)S(1)}, u32[]{:S(2)}, u32[]{:S(2)}) collective-permute-start(f32[5,16,128]{2,1,0:T(8,128)S(1)} %get-tuple-element.20), channel_id=1, source_target_pairs={{0,2},{2,0},{4,6},{6,4},{8,10},{10,8},{12,14},{14,12},{16,18},{18,... | collective-permute-start | bytes 122888 | tf_op jit(solution)/shard_map/ppermute | solution.py:308
  24.6 1.9 %collective-permute-done.4 = f32[5,16,128]{2,1,0:T(8,128)S(1)} collective-permute-done((f32[5,16,128]{2,1,0:T(8,128)S(1)}, f32[5,16,128]{2,1,0:T(8,128)S(1)}, u32[]{:S(2)}, u32[]{:S(2)}) %collective-permute-start.4) | collective-permute-done | bytes 40992 | tf_op jit(solution)/shard_map/ppermute | solution.py:308
  26.4 0.9 %collective-permute-done.5 = f32[5,16,128]{2,1,0:T(8,128)S(1)} collective-permute-done((f32[5,16,128]{2,1,0:T(8,128)S(1)}, f32[5,16,128]{2,1,0:T(8,128)S(1)}, u32[]{:S(2)}, u32[]{:S(2)}) %collective-permute-start.5) | collective-permute-done | bytes 40992 | tf_op jit(solution)/shard_map/ppermute | solution.py:308
  27.3 0.0 collective-permute-done.6
  27.3 0.9 %fisher.1 = (f32[1,128,512]{2,1,0:T(8,128)}, f32[2,4,512]{2,1,0:T(4,128)}) custom-call(f32[1,5,16,128]{3,2,1,0:T(8,128)S(1)} %bitcast.8, f32[1,5,16,128]{3,2,1,0:T(8,128)S(1)} %bitcast.9, f32[1,5,16,128]{3,2,1,0:T(8,128)S(1)} %bitcast.10, f32[1,5,16,128]{3,2,1,0:T(8,128)S(1)} %bitcast.11, f32[2,4,512]{2,1,0:T(4,128)S(1)} %get-tuple-element.21.refs_4_), custom_call_target="tpu_custom_call" | custom-call | tf_op jit(solution)/shard_map/fisher/pallas_call | solution.py:252
  (3 shorter events, 0.1 us)
Async XLA Ops:
  0.6 9.5 %copy-start.1 = (s32[16]{0:T(128)S(1)}, s32[16]{0:T(128)}, u32[]{:S(2)}) copy-start(s32[16]{0:T(128)} %param.19) | copy-start | bytes 196
  0.6 13.0 %copy-start = (s32[1,256]{1,0:T(1,128)S(1)}, s32[1,256]{1,0:T(1,128)}, u32[]{:S(2)}) copy-start(s32[1,256]{1,0:T(1,128)} %refs_2_.3) | copy-start | bytes 3076
  7.1 6.5 %collective-permute-start = (f32[2,128,128]{2,1,0:T(8,128)S(1)}, f32[2,128,128]{2,1,0:T(8,128)S(1)}, u32[]{:S(2)}, u32[]{:S(2)}) collective-permute-start(f32[2,128,128]{2,1,0:T(8,128)S(1)} %project.1.low_ref), channel_id=1, source_target_pairs={{0,1},{1,0},{2,3},{3,2},{4,5},{5,4},{6,7},{7,6},{8,9},{9,8},{10,11... | collective-permute-start | bytes 393224 | tf_op jit(solution)/shard_map/ppermute | solution.py:293
  14.0 5.8 %collective-permute-start.1 = (f32[12,4,128]{2,1,0:T(4,128)S(1)}, f32[12,4,128]{2,1,0:T(4,128)S(1)}, u32[]{:S(2)}, u32[]{:S(2)}) collective-permute-start(f32[12,4,128]{2,1,0:T(4,128)S(1)} %get-tuple-element.14), channel_id=1, source_target_pairs={{0,8},{2,10},{4,12},{6,14},{8,16},{10,18},{12,20},{14,22},{16,24},... | collective-permute-start | bytes 73736 | tf_op jit(solution)/shard_map/ppermute | solution.py:304
  15.9 4.7 %collective-permute-start.2 = (f32[12,4,128]{2,1,0:T(4,128)S(1)}, f32[12,4,128]{2,1,0:T(4,128)S(1)}, u32[]{:S(2)}, u32[]{:S(2)}) collective-permute-start(f32[12,4,128]{2,1,0:T(4,128)S(1)} %get-tuple-element.15), channel_id=1, source_target_pairs={{0,16},{2,18},{4,20},{6,22},{8,24},{10,26},{12,28},{14,30},{16,0},... | collective-permute-start | bytes 73736 | tf_op jit(solution)/shard_map/ppermute | solution.py:304
  18.5 3.8 %collective-permute-start.3 = (f32[12,4,128]{2,1,0:T(4,128)S(1)}, f32[12,4,128]{2,1,0:T(4,128)S(1)}, u32[]{:S(2)}, u32[]{:S(2)}) collective-permute-start(f32[12,4,128]{2,1,0:T(4,128)S(1)} %get-tuple-element.16), channel_id=1, source_target_pairs={{0,24},{2,26},{4,28},{6,30},{8,0},{10,2},{12,4},{14,6},{16,8},{18,... | collective-permute-start | bytes 73736 | tf_op jit(solution)/shard_map/ppermute | solution.py:304
  22.4 4.1 %collective-permute-start.4 = (f32[5,16,128]{2,1,0:T(8,128)S(1)}, f32[5,16,128]{2,1,0:T(8,128)S(1)}, u32[]{:S(2)}, u32[]{:S(2)}) collective-permute-start(f32[5,16,128]{2,1,0:T(8,128)S(1)} %get-tuple-element.18), channel_id=1, source_target_pairs={{0,4},{2,6},{4,0},{6,2},{8,12},{10,14},{12,8},{14,10},{16,20},{18,... | collective-permute-start | bytes 122888 | tf_op jit(solution)/shard_map/ppermute | solution.py:308
  23.9 3.4 %collective-permute-start.5 = (f32[5,16,128]{2,1,0:T(8,128)S(1)}, f32[5,16,128]{2,1,0:T(8,128)S(1)}, u32[]{:S(2)}, u32[]{:S(2)}) collective-permute-start(f32[5,16,128]{2,1,0:T(8,128)S(1)} %get-tuple-element.19), channel_id=1, source_target_pairs={{0,6},{2,4},{4,2},{6,0},{8,14},{10,12},{12,10},{14,8},{16,22},{18,... | collective-permute-start | bytes 122888 | tf_op jit(solution)/shard_map/ppermute | solution.py:308
  23.9 3.4 %collective-permute-start.6 = (f32[5,16,128]{2,1,0:T(8,128)S(1)}, f32[5,16,128]{2,1,0:T(8,128)S(1)}, u32[]{:S(2)}, u32[]{:S(2)}) collective-permute-start(f32[5,16,128]{2,1,0:T(8,128)S(1)} %get-tuple-element.20), channel_id=1, source_target_pairs={{0,2},{2,0},{4,6},{6,4},{8,10},{10,8},{12,14},{14,12},{16,18},{18,... | collective-permute-start | bytes 122888 | tf_op jit(solution)/shard_map/ppermute | solution.py:308

commit v7 on v6

--- a/solution.py
+++ b/solution.py
@@ -13,9 +13,8 @@
 NT = (((1,), (1,)), ((), ()))
 TN = (((0,), (0,)), ((), ()))
 PIECE = 4096
-PLANE = 4
-PLANE_SHIFTS = (2, 1, 3)
-PLANE_STEPS = (2, 3, 1)
+FIRST = (0, 3, 2, 1)
+SECOND = (0, 8, 12, 4)
 VMEM_BYTES = 54976 * 2**10
 SMALL_BYTES = 8 * 2**20
 
@@ -150,13 +149,13 @@
         for k in range(col_slabs):
             send_refs[0][j, 1 + k] = jnp.where(wanted < n_slabs, columns[0][k], columns[1][k])
     if n_sends > 1:
-        plane = lax.axis_index("dp") // PLANE
-        for shift, send_ref in enumerate(send_refs):
+        me = lax.axis_index("dp")
+        for target, send_ref in zip(FIRST, send_refs):
             for p in range(2):
                 for k in range(col_slabs):
                     send_ref[p * col_slabs + k] = columns[p][k]
-            for d in range(PLANE):
-                send_ref[2 * col_slabs + d] = refs[-1][lax.rem(plane + shift, n_sends) * PLANE + d]
+            for d, step in enumerate(SECOND):
+                send_ref[2 * col_slabs + d] = refs[-1][me ^ target ^ step]
 
 
 def vectors(parts, segments, wanted, col_width, sends):
@@ -178,29 +177,27 @@
 
 
 def regroup_kernel(n_slabs, *refs):
-    blocks, wanted_ref, outs = refs[: len(refs) // 2], refs[len(refs) // 2], refs[len(refs) // 2 + 1 :]
-    col_slabs = (blocks[0].shape[0] - PLANE) // 2
+    blocks, wanted_ref, outs = refs[: len(FIRST)], refs[len(FIRST)], refs[len(FIRST) + 1 :]
+    col_slabs = (blocks[0].shape[0] - len(SECOND)) // 2
     me = lax.axis_index("dp")
-    plane, place = me // PLANE, lax.rem(me, PLANE)
-    for step, out in zip((0,) + PLANE_STEPS, outs):
-        target = place ^ step
-        first = wanted_ref[plane * PLANE + target] < n_slabs
+    for d, (step, out) in enumerate(zip(SECOND, outs)):
+        first = wanted_ref[me ^ step] < n_slabs
         for i, block in enumerate(blocks):
             rows = pl.ds(i * EX_DEV, EX_DEV)
-            out[0, rows, :] = block[2 * col_slabs + target]
+            out[0, rows, :] = block[2 * col_slabs + d]
             for k in range(col_slabs):
                 out[1 + k, rows, :] = jnp.where(first, block[k], block[col_slabs + k])
 
 
 def regroup(blocks, wanted, n_slabs):
-    col_slabs = (blocks[0].shape[0] - PLANE) // 2
+    col_slabs = (blocks[0].shape[0] - len(SECOND)) // 2
     vmem = pl.BlockSpec(memory_space=pltpu.VMEM)
     part = jax.ShapeDtypeStruct((1 + col_slabs, len(blocks) * EX_DEV, LANES), jnp.float32)
     return pl.pallas_call(
         functools.partial(regroup_kernel, n_slabs),
-        out_shape=[part] * PLANE,
+        out_shape=[part] * len(SECOND),
         in_specs=[vmem] * (len(blocks) + 1),
-        out_specs=[vmem] * PLANE,
+        out_specs=[vmem] * len(SECOND),
         compiler_params=pltpu.CompilerParams(vmem_limit_bytes=SMALL_BYTES),
         name="regroup",
     )(*blocks, wanted)
@@ -295,17 +292,14 @@
         parts = (lax.psum(own, "tensor"),)
     wanted = jnp.broadcast_to((owner_map * own_rows // LANES)[:, None, None], (dp_count, EX_DEV, LANES))
     col_slabs = col_width // LANES
-    planes = dp_count // PLANE
-    if planes == 4 and own_rows == LANES:
-        block = (2 * col_slabs + PLANE,)
-        vec, *blocks = vectors(parts, segment_ids, wanted, col_width, [block] * planes)
-        for shift in PLANE_SHIFTS:
-            pairs = [(i, (i + shift * PLANE) % dp_count) for i in range(dp_count)]
-            blocks[shift] = lax.ppermute(blocks[shift], "dp", pairs)
-        grouped = regroup(blocks, wanted, width // LANES)
-        recv = [grouped[0]]
-        for part, step in zip(grouped[1:], PLANE_STEPS):
-            recv.append(lax.ppermute(part, "dp", [(i, i ^ step) for i in range(dp_count)]))
+    if dp_count == len(FIRST) * len(SECOND) and own_rows == LANES:
+        block = (2 * col_slabs + len(SECOND),)
+        vec, *blocks = vectors(parts, segment_ids, wanted, col_width, [block] * len(FIRST))
+        for n, step in enumerate(FIRST[1:], 1):
+            blocks[n] = lax.ppermute(blocks[n], "dp", [(i, i ^ step) for i in range(dp_count)])
+        recv = list(regroup(blocks, wanted, width // LANES))
+        for n, step in enumerate(SECOND[1:], 1):
+            recv[n] = lax.ppermute(recv[n], "dp", [(i, i ^ step) for i in range(dp_count)])
         recv = [part[None] for part in recv]
     else:
         vec, send = vectors(parts, segment_ids, wanted, col_width, [(dp_count, 1 + col_slabs)])

time: 28.4 us -> 27.9 us (0.982)
  starting transfers between devices: 11 us -> 9.23 us
  waiting for transfers between devices: 8.7 us -> 9.94 us
    ppermute x6, starting transfers between devices: 7.99 us -> 6.19 us  [the longest x3 4.25 us: shards(): lax.ppermute(recv[n], 'dp', [(i, i ^ step) for i in range(dp_count)])]
    ppermute x6, waiting for transfers between devices: 5.24 us -> 6.48 us  [the longest x3 4.23 us: shards(): lax.ppermute(recv[n], 'dp', [(i, i ^ step) for i in range(dp_count)])]
where the time goes in v7:
time: 27.9 us; the launch traced here: 27.7 us
  waiting for transfers between devices  9.94 us (36%)
  starting transfers between devices  9.23 us (33%)
  Pallas kernels  7.75 us (28%)
  between operations  0.7 us (3%)
    pallas_call x1, Pallas kernels, project(): pl.pallas_call(functools.partial(project_kernel, plan, halves), out_shape...  6.4 us
    ppermute x3, starting transfers between devices, shards(): lax.ppermute(recv[n], 'dp', [(i, i ^ step) for i in range(dp_count)])  4.25 us
    ppermute x3, waiting for transfers between devices, shards(): lax.ppermute(recv[n], 'dp', [(i, i ^ step) for i in range(dp_count)])  4.23 us
    ppermute x1, waiting for transfers between devices, shards(): parts = (stage(own), lax.ppermute(own, 'tensor', [(0, 1), (1, 0)]))  3.46 us
    ppermute x1, starting transfers between devices, shards(): parts = (stage(own), lax.ppermute(own, 'tensor', [(0, 1), (1, 0)]))  3.03 us
    ppermute x3, waiting for transfers between devices, shards(): lax.ppermute(blocks[n], 'dp', [(i, i ^ step) for i in range(dp_count)])  2.25 us
    ppermute x3, starting transfers between devices, shards(): lax.ppermute(blocks[n], 'dp', [(i, i ^ step) for i in range(dp_count)])  1.94 us
    pallas_call x1, Pallas kernels, fisher(): pl.pallas_call(functools.partial(fisher_kernel, 1.0 / examples, len(parts...  0.94 us
  transfers between devices with their start and end apart: 7, of which 5 were waited for; matrix products, arithmetic and copies ran while one was open for 0% of the time, Pallas kernels for 0%

profile of v7, /device:TPU:0, one launch (start us, length us, event | category | flops | bytes accessed | tf_op | source)
XLA Modules:
  0.0 27.7 jit_solution(7485008469003392156)
XLA Ops:
  0.6 0.0 copy-start.1
  0.6 0.0 copy-start
  0.7 6.4 %project.1.low_ref = f32[2,128,128]{2,1,0:T(8,128)S(1)} custom-call(bf16[256,4096]{1,0:T(8,128)(2,1)} %refs_0_.1, bf16[256,4096]{1,0:T(8,128)(2,1)} %refs_1_.1, bf16[256,4096]{1,0:T(8,128)(2,1)} %refs_2_.2, bf16[256,14336]{1,0:T(8,128)(2,1)} %refs_3_.1, bf16[32,4096]{1,0:T(8,128)(2,1)} %bitcast.13, bf16[32,4096]{1,0:T(8,128)(2,1)} %bitcast.14, ...), custom_call_target="tpu_custom_call" | custom-call | tf_op jit(solution)/shard_map/project/pallas_call | solution.py:71
  7.1 3.0 %collective-permute-start = (f32[2,128,128]{2,1,0:T(8,128)S(1)}, f32[2,128,128]{2,1,0:T(8,128)S(1)}, u32[]{:S(2)}, u32[]{:S(2)}) collective-permute-start(f32[2,128,128]{2,1,0:T(8,128)S(1)} %project.1.low_ref), channel_id=1, source_target_pairs={{0,1},{1,0},{2,3},{3,2},{4,5},{5,4},{6,7},{7,6},{8,9},{9,8},{10,11... | collective-permute-start | bytes 393224 | tf_op jit(solution)/shard_map/ppermute | solution.py:290
  10.1 0.0 copy-done.1
  10.1 3.5 %collective-permute-done.refs_1_ = f32[2,128,128]{2,1,0:T(8,128)S(1)} collective-permute-done((f32[2,128,128]{2,1,0:T(8,128)S(1)}, f32[2,128,128]{2,1,0:T(8,128)S(1)}, u32[]{:S(2)}, u32[]{:S(2)}) %collective-permute-start) | collective-permute-done | bytes 131104 | tf_op jit(solution)/shard_map/ppermute | solution.py:290
  13.6 0.1 broadcast_in_dim.18.refs_3_.refs_4_
  13.7 0.0 copy-done
  13.7 0.4 %vectors.1 = (f32[2,4,512]{2,1,0:T(4,128)S(1)}, f32[12,4,128]{2,1,0:T(4,128)S(1)}, f32[12,4,128]{2,1,0:T(4,128)S(1)}, f32[12,4,128]{2,1,0:T(4,128)S(1)}, f32[12,4,128]{2,1,0:T(4,128)S(1)}) custom-call(f32[2,128,128]{2,1,0:T(8,128)S(1)} %stage.1.refs_0_, f32[2,128,128]{2,1,0:T(8,128)S(1)} %collective-permute-done.refs_1_, s32[1,256]{1,0:T(1,128)S(1)} %copy-done, ...), custom_call_target="tpu_custom_call" | custom-call | tf_op jit(solution)/shard_map/vectors/pallas_call | solution.py:164
  14.1 0.4 %collective-permute-start.1 = (f32[12,4,128]{2,1,0:T(4,128)S(1)}, f32[12,4,128]{2,1,0:T(4,128)S(1)}, u32[]{:S(2)}, u32[]{:S(2)}) collective-permute-start(f32[12,4,128]{2,1,0:T(4,128)S(1)} %get-tuple-element.14), channel_id=1, source_target_pairs={{0,6},{2,4},{4,2},{6,0},{8,14},{10,12},{12,10},{14,8},{16,22},{18,... | collective-permute-start | bytes 73736 | tf_op jit(solution)/shard_map/ppermute | solution.py:299
  14.4 1.5 %collective-permute-start.2 = (f32[12,4,128]{2,1,0:T(4,128)S(1)}, f32[12,4,128]{2,1,0:T(4,128)S(1)}, u32[]{:S(2)}, u32[]{:S(2)}) collective-permute-start(f32[12,4,128]{2,1,0:T(4,128)S(1)} %get-tuple-element.15), channel_id=1, source_target_pairs={{0,4},{2,6},{4,0},{6,2},{8,12},{10,14},{12,8},{14,10},{16,20},{18,... | collective-permute-start | bytes 73736 | tf_op jit(solution)/shard_map/ppermute | solution.py:299
  15.9 0.1 collective-permute-start.3
  16.0 1.4 %collective-permute-done.1.refs_1_ = f32[12,4,128]{2,1,0:T(4,128)S(1)} collective-permute-done((f32[12,4,128]{2,1,0:T(4,128)S(1)}, f32[12,4,128]{2,1,0:T(4,128)S(1)}, u32[]{:S(2)}, u32[]{:S(2)}) %collective-permute-start.1) | collective-permute-done | bytes 24608 | tf_op jit(solution)/shard_map/ppermute | solution.py:299
  17.4 0.9 %collective-permute-done.2.refs_2_ = f32[12,4,128]{2,1,0:T(4,128)S(1)} collective-permute-done((f32[12,4,128]{2,1,0:T(4,128)S(1)}, f32[12,4,128]{2,1,0:T(4,128)S(1)}, u32[]{:S(2)}, u32[]{:S(2)}) %collective-permute-start.2) | collective-permute-done | bytes 24608 | tf_op jit(solution)/shard_map/ppermute | solution.py:299
  18.2 0.0 collective-permute-done.3.refs_3_
  18.3 2.7 %collective-permute-start.4 = (f32[5,16,128]{2,1,0:T(8,128)S(1)}, f32[5,16,128]{2,1,0:T(8,128)S(1)}, u32[]{:S(2)}, u32[]{:S(2)}) collective-permute-start(f32[5,16,128]{2,1,0:T(8,128)S(1)} %get-tuple-element.18), channel_id=1, source_target_pairs={{0,16},{2,18},{4,20},{6,22},{8,24},{10,26},{12,28},{14,30},{16,0},... | collective-permute-start | bytes 122888 | tf_op jit(solution)/shard_map/ppermute | solution.py:302
  21.0 1.3 %collective-permute-start.5 = (f32[5,16,128]{2,1,0:T(8,128)S(1)}, f32[5,16,128]{2,1,0:T(8,128)S(1)}, u32[]{:S(2)}, u32[]{:S(2)}) collective-permute-start(f32[5,16,128]{2,1,0:T(8,128)S(1)} %get-tuple-element.19), channel_id=1, source_target_pairs={{0,24},{2,26},{4,28},{6,30},{8,16},{10,18},{12,20},{14,22},{16,8},... | collective-permute-start | bytes 122888 | tf_op jit(solution)/shard_map/ppermute | solution.py:302
  22.3 0.2 collective-permute-start.6
  22.5 0.7 %collective-permute-done.4 = f32[5,16,128]{2,1,0:T(8,128)S(1)} collective-permute-done((f32[5,16,128]{2,1,0:T(8,128)S(1)}, f32[5,16,128]{2,1,0:T(8,128)S(1)}, u32[]{:S(2)}, u32[]{:S(2)}) %collective-permute-start.4) | collective-permute-done | bytes 40992 | tf_op jit(solution)/shard_map/ppermute | solution.py:302
  23.3 3.5 %collective-permute-done.5 = f32[5,16,128]{2,1,0:T(8,128)S(1)} collective-permute-done((f32[5,16,128]{2,1,0:T(8,128)S(1)}, f32[5,16,128]{2,1,0:T(8,128)S(1)}, u32[]{:S(2)}, u32[]{:S(2)}) %collective-permute-start.5) | collective-permute-done | bytes 40992 | tf_op jit(solution)/shard_map/ppermute | solution.py:302
  26.8 0.0 collective-permute-done.6
  26.8 0.9 %fisher.1 = (f32[1,128,512]{2,1,0:T(8,128)}, f32[2,4,512]{2,1,0:T(4,128)}) custom-call(f32[1,5,16,128]{3,2,1,0:T(8,128)S(1)} %bitcast.8, f32[1,5,16,128]{3,2,1,0:T(8,128)S(1)} %bitcast.9, f32[1,5,16,128]{3,2,1,0:T(8,128)S(1)} %bitcast.10, f32[1,5,16,128]{3,2,1,0:T(8,128)S(1)} %bitcast.11, f32[2,4,512]{2,1,0:T(4,128)S(1)} %get-tuple-element.21.refs_4_), custom_call_target="tpu_custom_call" | custom-call | tf_op jit(solution)/shard_map/fisher/pallas_call | solution.py:249
  (3 shorter events, 0.1 us)
Async XLA Ops:
  0.6 9.5 %copy-start.1 = (s32[16]{0:T(128)S(1)}, s32[16]{0:T(128)}, u32[]{:S(2)}) copy-start(s32[16]{0:T(128)} %param.19) | copy-start | bytes 196
  0.6 13.0 %copy-start = (s32[1,256]{1,0:T(1,128)S(1)}, s32[1,256]{1,0:T(1,128)}, u32[]{:S(2)}) copy-start(s32[1,256]{1,0:T(1,128)} %refs_2_.3) | copy-start | bytes 3076
  7.1 6.5 %collective-permute-start = (f32[2,128,128]{2,1,0:T(8,128)S(1)}, f32[2,128,128]{2,1,0:T(8,128)S(1)}, u32[]{:S(2)}, u32[]{:S(2)}) collective-permute-start(f32[2,128,128]{2,1,0:T(8,128)S(1)} %project.1.low_ref), channel_id=1, source_target_pairs={{0,1},{1,0},{2,3},{3,2},{4,5},{5,4},{6,7},{7,6},{8,9},{9,8},{10,11... | collective-permute-start | bytes 393224 | tf_op jit(solution)/shard_map/ppermute | solution.py:290
  14.1 3.3 %collective-permute-start.1 = (f32[12,4,128]{2,1,0:T(4,128)S(1)}, f32[12,4,128]{2,1,0:T(4,128)S(1)}, u32[]{:S(2)}, u32[]{:S(2)}) collective-permute-start(f32[12,4,128]{2,1,0:T(4,128)S(1)} %get-tuple-element.14), channel_id=1, source_target_pairs={{0,6},{2,4},{4,2},{6,0},{8,14},{10,12},{12,10},{14,8},{16,22},{18,... | collective-permute-start | bytes 73736 | tf_op jit(solution)/shard_map/ppermute | solution.py:299
  14.4 3.8 %collective-permute-start.2 = (f32[12,4,128]{2,1,0:T(4,128)S(1)}, f32[12,4,128]{2,1,0:T(4,128)S(1)}, u32[]{:S(2)}, u32[]{:S(2)}) collective-permute-start(f32[12,4,128]{2,1,0:T(4,128)S(1)} %get-tuple-element.15), channel_id=1, source_target_pairs={{0,4},{2,6},{4,0},{6,2},{8,12},{10,14},{12,8},{14,10},{16,20},{18,... | collective-permute-start | bytes 73736 | tf_op jit(solution)/shard_map/ppermute | solution.py:299
  15.9 2.3 %collective-permute-start.3 = (f32[12,4,128]{2,1,0:T(4,128)S(1)}, f32[12,4,128]{2,1,0:T(4,128)S(1)}, u32[]{:S(2)}, u32[]{:S(2)}) collective-permute-start(f32[12,4,128]{2,1,0:T(4,128)S(1)} %get-tuple-element.16), channel_id=1, source_target_pairs={{0,2},{2,0},{4,6},{6,4},{8,10},{10,8},{12,14},{14,12},{16,18},{18,... | collective-permute-start | bytes 73736 | tf_op jit(solution)/shard_map/ppermute | solution.py:299
  18.3 5.0 %collective-permute-start.4 = (f32[5,16,128]{2,1,0:T(8,128)S(1)}, f32[5,16,128]{2,1,0:T(8,128)S(1)}, u32[]{:S(2)}, u32[]{:S(2)}) collective-permute-start(f32[5,16,128]{2,1,0:T(8,128)S(1)} %get-tuple-element.18), channel_id=1, source_target_pairs={{0,16},{2,18},{4,20},{6,22},{8,24},{10,26},{12,28},{14,30},{16,0},... | collective-permute-start | bytes 122888 | tf_op jit(solution)/shard_map/ppermute | solution.py:302
  21.0 5.8 %collective-permute-start.5 = (f32[5,16,128]{2,1,0:T(8,128)S(1)}, f32[5,16,128]{2,1,0:T(8,128)S(1)}, u32[]{:S(2)}, u32[]{:S(2)}) collective-permute-start(f32[5,16,128]{2,1,0:T(8,128)S(1)} %get-tuple-element.19), channel_id=1, source_target_pairs={{0,24},{2,26},{4,28},{6,30},{8,16},{10,18},{12,20},{14,22},{16,8},... | collective-permute-start | bytes 122888 | tf_op jit(solution)/shard_map/ppermute | solution.py:302
  22.3 4.5 %collective-permute-start.6 = (f32[5,16,128]{2,1,0:T(8,128)S(1)}, f32[5,16,128]{2,1,0:T(8,128)S(1)}, u32[]{:S(2)}, u32[]{:S(2)}) collective-permute-start(f32[5,16,128]{2,1,0:T(8,128)S(1)} %get-tuple-element.20), channel_id=1, source_target_pairs={{0,8},{2,10},{4,12},{6,14},{8,0},{10,2},{12,4},{14,6},{16,24},{18,... | collective-permute-start | bytes 122888 | tf_op jit(solution)/shard_map/ppermute | solution.py:302

commit v8 on v7

--- a/solution.py
+++ b/solution.py
@@ -14,7 +14,8 @@
 TN = (((0,), (0,)), ((), ()))
 PIECE = 4096
 FIRST = (0, 3, 2, 1)
-SECOND = (0, 8, 12, 4)
+SECOND = (0, 4, 8, 12)
+LAST = len(FIRST) * len(SECOND) - 1
 VMEM_BYTES = 54976 * 2**10
 SMALL_BYTES = 8 * 2**20
 
@@ -155,7 +156,7 @@
                 for k in range(col_slabs):
                     send_ref[p * col_slabs + k] = columns[p][k]
             for d, step in enumerate(SECOND):
-                send_ref[2 * col_slabs + d] = refs[-1][me ^ target ^ step]
+                send_ref[2 * col_slabs + d] = refs[-1][((me ^ target) + step) & LAST]
 
 
 def vectors(parts, segments, wanted, col_width, sends):
@@ -181,7 +182,7 @@
     col_slabs = (blocks[0].shape[0] - len(SECOND)) // 2
     me = lax.axis_index("dp")
     for d, (step, out) in enumerate(zip(SECOND, outs)):
-        first = wanted_ref[me ^ step] < n_slabs
+        first = wanted_ref[(me + step) & LAST] < n_slabs
         for i, block in enumerate(blocks):
             rows = pl.ds(i * EX_DEV, EX_DEV)
             out[0, rows, :] = block[2 * col_slabs + d]
@@ -299,7 +300,7 @@
             blocks[n] = lax.ppermute(blocks[n], "dp", [(i, i ^ step) for i in range(dp_count)])
         recv = list(regroup(blocks, wanted, width // LANES))
         for n, step in enumerate(SECOND[1:], 1):
-            recv[n] = lax.ppermute(recv[n], "dp", [(i, i ^ step) for i in range(dp_count)])
+            recv[n] = lax.ppermute(recv[n], "dp", [(i, (i + step) & LAST) for i in range(dp_count)])
         recv = [part[None] for part in recv]
     else:
         vec, send = vectors(parts, segment_ids, wanted, col_width, [(dp_count, 1 + col_slabs)])

time: 27.9 us -> 27.6 us (0.989)
  waiting for transfers between devices: 9.94 us -> 8.39 us
  starting transfers between devices: 9.23 us -> 10.6 us
    ppermute x3, waiting for transfers between devices: 4.23 us -> 2.68 us  [shards(): lax.ppermute(recv[n], 'dp', [(i, i + step & LAST) for i in range(dp_count)])]
    ppermute x3, starting transfers between devices: 4.25 us -> 5.59 us  [shards(): lax.ppermute(recv[n], 'dp', [(i, i + step & LAST) for i in range(dp_count)])]
  transfers between devices with their start and end apart: 7 -> 7, of which waited for: 5 -> 6; matrix products, arithmetic and copies ran while one was open for 0% -> 0% of each run, Pallas kernels for 0% -> 0%
where the time goes in v8:
time: 27.6 us; the launch traced here: 27.5 us
  starting transfers between devices  10.6 us (38%)
  waiting for transfers between devices  8.39 us (30%)
  Pallas kernels  7.75 us (28%)
  between operations  0.7 us (3%)
    pallas_call x1, Pallas kernels, project(): pl.pallas_call(functools.partial(project_kernel, plan, halves), out_shape...  6.4 us
    ppermute x3, starting transfers between devices, shards(): lax.ppermute(recv[n], 'dp', [(i, i + step & LAST) for i in range(dp_count)])  5.59 us
    ppermute x1, waiting for transfers between devices, shards(): parts = (stage(own), lax.ppermute(own, 'tensor', [(0, 1), (1, 0)]))  3.46 us
    ppermute x1, starting transfers between devices, shards(): parts = (stage(own), lax.ppermute(own, 'tensor', [(0, 1), (1, 0)]))  3.03 us
    ppermute x3, waiting for transfers between devices, shards(): lax.ppermute(recv[n], 'dp', [(i, i + step & LAST) for i in range(dp_count)])  2.68 us
    ppermute x3, waiting for transfers between devices, shards(): lax.ppermute(blocks[n], 'dp', [(i, i ^ step) for i in range(dp_count)])  2.25 us
    ppermute x3, starting transfers between devices, shards(): lax.ppermute(blocks[n], 'dp', [(i, i ^ step) for i in range(dp_count)])  1.94 us
    pallas_call x1, Pallas kernels, fisher(): pl.pallas_call(functools.partial(fisher_kernel, 1.0 / examples, len(parts...  0.94 us
  transfers between devices with their start and end apart: 7, of which 6 were waited for; matrix products, arithmetic and copies ran while one was open for 0% of the time, Pallas kernels for 0%

profile of v8, /device:TPU:0, one launch (start us, length us, event | category | flops | bytes accessed | tf_op | source)
XLA Modules:
  0.0 27.5 jit_solution(11944699797700936445)
XLA Ops:
  0.6 0.0 copy-start.1
  0.6 0.0 copy-start
  0.7 6.4 %project.1.low_ref = f32[2,128,128]{2,1,0:T(8,128)S(1)} custom-call(bf16[256,4096]{1,0:T(8,128)(2,1)} %refs_0_.1, bf16[256,4096]{1,0:T(8,128)(2,1)} %refs_1_.1, bf16[256,4096]{1,0:T(8,128)(2,1)} %refs_2_.2, bf16[256,14336]{1,0:T(8,128)(2,1)} %refs_3_.1, bf16[32,4096]{1,0:T(8,128)(2,1)} %bitcast.13, bf16[32,4096]{1,0:T(8,128)(2,1)} %bitcast.14, ...), custom_call_target="tpu_custom_call" | custom-call | tf_op jit(solution)/shard_map/project/pallas_call | solution.py:72
  7.1 3.0 %collective-permute-start = (f32[2,128,128]{2,1,0:T(8,128)S(1)}, f32[2,128,128]{2,1,0:T(8,128)S(1)}, u32[]{:S(2)}, u32[]{:S(2)}) collective-permute-start(f32[2,128,128]{2,1,0:T(8,128)S(1)} %project.1.low_ref), channel_id=1, source_target_pairs={{0,1},{1,0},{2,3},{3,2},{4,5},{5,4},{6,7},{7,6},{8,9},{9,8},{10,11... | collective-permute-start | bytes 393224 | tf_op jit(solution)/shard_map/ppermute | solution.py:291
  10.1 0.0 copy-done.1
  10.1 3.5 %collective-permute-done.refs_1_ = f32[2,128,128]{2,1,0:T(8,128)S(1)} collective-permute-done((f32[2,128,128]{2,1,0:T(8,128)S(1)}, f32[2,128,128]{2,1,0:T(8,128)S(1)}, u32[]{:S(2)}, u32[]{:S(2)}) %collective-permute-start) | collective-permute-done | bytes 131104 | tf_op jit(solution)/shard_map/ppermute | solution.py:291
  13.6 0.1 broadcast_in_dim.18.refs_3_.refs_4_
  13.7 0.0 copy-done
  13.7 0.4 %vectors.1 = (f32[2,4,512]{2,1,0:T(4,128)S(1)}, f32[12,4,128]{2,1,0:T(4,128)S(1)}, f32[12,4,128]{2,1,0:T(4,128)S(1)}, f32[12,4,128]{2,1,0:T(4,128)S(1)}, f32[12,4,128]{2,1,0:T(4,128)S(1)}) custom-call(f32[2,128,128]{2,1,0:T(8,128)S(1)} %stage.1.refs_0_, f32[2,128,128]{2,1,0:T(8,128)S(1)} %collective-permute-done.refs_1_, s32[1,256]{1,0:T(1,128)S(1)} %copy-done, ...), custom_call_target="tpu_custom_call" | custom-call | tf_op jit(solution)/shard_map/vectors/pallas_call | solution.py:165
  14.1 0.4 %collective-permute-start.1 = (f32[12,4,128]{2,1,0:T(4,128)S(1)}, f32[12,4,128]{2,1,0:T(4,128)S(1)}, u32[]{:S(2)}, u32[]{:S(2)}) collective-permute-start(f32[12,4,128]{2,1,0:T(4,128)S(1)} %get-tuple-element.14), channel_id=1, source_target_pairs={{0,6},{2,4},{4,2},{6,0},{8,14},{10,12},{12,10},{14,8},{16,22},{18,... | collective-permute-start | bytes 73736 | tf_op jit(solution)/shard_map/ppermute | solution.py:300
  14.4 1.5 %collective-permute-start.2 = (f32[12,4,128]{2,1,0:T(4,128)S(1)}, f32[12,4,128]{2,1,0:T(4,128)S(1)}, u32[]{:S(2)}, u32[]{:S(2)}) collective-permute-start(f32[12,4,128]{2,1,0:T(4,128)S(1)} %get-tuple-element.15), channel_id=1, source_target_pairs={{0,4},{2,6},{4,0},{6,2},{8,12},{10,14},{12,8},{14,10},{16,20},{18,... | collective-permute-start | bytes 73736 | tf_op jit(solution)/shard_map/ppermute | solution.py:300
  15.9 0.1 collective-permute-start.3
  16.0 1.4 %collective-permute-done.1.refs_1_ = f32[12,4,128]{2,1,0:T(4,128)S(1)} collective-permute-done((f32[12,4,128]{2,1,0:T(4,128)S(1)}, f32[12,4,128]{2,1,0:T(4,128)S(1)}, u32[]{:S(2)}, u32[]{:S(2)}) %collective-permute-start.1) | collective-permute-done | bytes 24608 | tf_op jit(solution)/shard_map/ppermute | solution.py:300
  17.4 0.9 %collective-permute-done.2.refs_2_ = f32[12,4,128]{2,1,0:T(4,128)S(1)} collective-permute-done((f32[12,4,128]{2,1,0:T(4,128)S(1)}, f32[12,4,128]{2,1,0:T(4,128)S(1)}, u32[]{:S(2)}, u32[]{:S(2)}) %collective-permute-start.2) | collective-permute-done | bytes 24608 | tf_op jit(solution)/shard_map/ppermute | solution.py:300
  18.2 0.0 collective-permute-done.3.refs_3_
  18.3 1.6 %collective-permute-start.4 = (f32[5,16,128]{2,1,0:T(8,128)S(1)}, f32[5,16,128]{2,1,0:T(8,128)S(1)}, u32[]{:S(2)}, u32[]{:S(2)}) collective-permute-start(f32[5,16,128]{2,1,0:T(8,128)S(1)} %get-tuple-element.18), channel_id=1, source_target_pairs={{0,8},{2,10},{4,12},{6,14},{8,16},{10,18},{12,20},{14,22},{16,24},... | collective-permute-start | bytes 122888 | tf_op jit(solution)/shard_map/ppermute | solution.py:303
  19.9 2.6 %collective-permute-start.5 = (f32[5,16,128]{2,1,0:T(8,128)S(1)}, f32[5,16,128]{2,1,0:T(8,128)S(1)}, u32[]{:S(2)}, u32[]{:S(2)}) collective-permute-start(f32[5,16,128]{2,1,0:T(8,128)S(1)} %get-tuple-element.19), channel_id=1, source_target_pairs={{0,16},{2,18},{4,20},{6,22},{8,24},{10,26},{12,28},{14,30},{16,0},... | collective-permute-start | bytes 122888 | tf_op jit(solution)/shard_map/ppermute | solution.py:303
  22.5 1.3 %collective-permute-start.6 = (f32[5,16,128]{2,1,0:T(8,128)S(1)}, f32[5,16,128]{2,1,0:T(8,128)S(1)}, u32[]{:S(2)}, u32[]{:S(2)}) collective-permute-start(f32[5,16,128]{2,1,0:T(8,128)S(1)} %get-tuple-element.20), channel_id=1, source_target_pairs={{0,24},{2,26},{4,28},{6,30},{8,0},{10,2},{12,4},{14,6},{16,8},{18,... | collective-permute-start | bytes 122888 | tf_op jit(solution)/shard_map/ppermute | solution.py:303
  23.9 0.3 %collective-permute-done.4 = f32[5,16,128]{2,1,0:T(8,128)S(1)} collective-permute-done((f32[5,16,128]{2,1,0:T(8,128)S(1)}, f32[5,16,128]{2,1,0:T(8,128)S(1)}, u32[]{:S(2)}, u32[]{:S(2)}) %collective-permute-start.4) | collective-permute-done | bytes 40992 | tf_op jit(solution)/shard_map/ppermute | solution.py:303
  24.2 2.0 %collective-permute-done.5 = f32[5,16,128]{2,1,0:T(8,128)S(1)} collective-permute-done((f32[5,16,128]{2,1,0:T(8,128)S(1)}, f32[5,16,128]{2,1,0:T(8,128)S(1)}, u32[]{:S(2)}, u32[]{:S(2)}) %collective-permute-start.5) | collective-permute-done | bytes 40992 | tf_op jit(solution)/shard_map/ppermute | solution.py:303
  26.1 0.4 %collective-permute-done.6 = f32[5,16,128]{2,1,0:T(8,128)S(1)} collective-permute-done((f32[5,16,128]{2,1,0:T(8,128)S(1)}, f32[5,16,128]{2,1,0:T(8,128)S(1)}, u32[]{:S(2)}, u32[]{:S(2)}) %collective-permute-start.6) | collective-permute-done | bytes 40992 | tf_op jit(solution)/shard_map/ppermute | solution.py:303
  26.5 0.9 %fisher.1 = (f32[1,128,512]{2,1,0:T(8,128)}, f32[2,4,512]{2,1,0:T(4,128)}) custom-call(f32[1,5,16,128]{3,2,1,0:T(8,128)S(1)} %bitcast.8, f32[1,5,16,128]{3,2,1,0:T(8,128)S(1)} %bitcast.9, f32[1,5,16,128]{3,2,1,0:T(8,128)S(1)} %bitcast.10, f32[1,5,16,128]{3,2,1,0:T(8,128)S(1)} %bitcast.11, f32[2,4,512]{2,1,0:T(4,128)S(1)} %get-tuple-element.21.refs_4_), custom_call_target="tpu_custom_call" | custom-call | tf_op jit(solution)/shard_map/fisher/pallas_call | solution.py:250
  (3 shorter events, 0.1 us)
Async XLA Ops:
  0.6 9.5 %copy-start.1 = (s32[16]{0:T(128)S(1)}, s32[16]{0:T(128)}, u32[]{:S(2)}) copy-start(s32[16]{0:T(128)} %param.19) | copy-start | bytes 196
  0.6 13.0 %copy-start = (s32[1,256]{1,0:T(1,128)S(1)}, s32[1,256]{1,0:T(1,128)}, u32[]{:S(2)}) copy-start(s32[1,256]{1,0:T(1,128)} %refs_2_.3) | copy-start | bytes 3076
  7.1 6.5 %collective-permute-start = (f32[2,128,128]{2,1,0:T(8,128)S(1)}, f32[2,128,128]{2,1,0:T(8,128)S(1)}, u32[]{:S(2)}, u32[]{:S(2)}) collective-permute-start(f32[2,128,128]{2,1,0:T(8,128)S(1)} %project.1.low_ref), channel_id=1, source_target_pairs={{0,1},{1,0},{2,3},{3,2},{4,5},{5,4},{6,7},{7,6},{8,9},{9,8},{10,11... | collective-permute-start | bytes 393224 | tf_op jit(solution)/shard_map/ppermute | solution.py:291
  14.1 3.3 %collective-permute-start.1 = (f32[12,4,128]{2,1,0:T(4,128)S(1)}, f32[12,4,128]{2,1,0:T(4,128)S(1)}, u32[]{:S(2)}, u32[]{:S(2)}) collective-permute-start(f32[12,4,128]{2,1,0:T(4,128)S(1)} %get-tuple-element.14), channel_id=1, source_target_pairs={{0,6},{2,4},{4,2},{6,0},{8,14},{10,12},{12,10},{14,8},{16,22},{18,... | collective-permute-start | bytes 73736 | tf_op jit(solution)/shard_map/ppermute | solution.py:300
  14.4 3.8 %collective-permute-start.2 = (f32[12,4,128]{2,1,0:T(4,128)S(1)}, f32[12,4,128]{2,1,0:T(4,128)S(1)}, u32[]{:S(2)}, u32[]{:S(2)}) collective-permute-start(f32[12,4,128]{2,1,0:T(4,128)S(1)} %get-tuple-element.15), channel_id=1, source_target_pairs={{0,4},{2,6},{4,0},{6,2},{8,12},{10,14},{12,8},{14,10},{16,20},{18,... | collective-permute-start | bytes 73736 | tf_op jit(solution)/shard_map/ppermute | solution.py:300
  15.9 2.3 %collective-permute-start.3 = (f32[12,4,128]{2,1,0:T(4,128)S(1)}, f32[12,4,128]{2,1,0:T(4,128)S(1)}, u32[]{:S(2)}, u32[]{:S(2)}) collective-permute-start(f32[12,4,128]{2,1,0:T(4,128)S(1)} %get-tuple-element.16), channel_id=1, source_target_pairs={{0,2},{2,0},{4,6},{6,4},{8,10},{10,8},{12,14},{14,12},{16,18},{18,... | collective-permute-start | bytes 73736 | tf_op jit(solution)/shard_map/ppermute | solution.py:300
  18.3 5.9 %collective-permute-start.4 = (f32[5,16,128]{2,1,0:T(8,128)S(1)}, f32[5,16,128]{2,1,0:T(8,128)S(1)}, u32[]{:S(2)}, u32[]{:S(2)}) collective-permute-start(f32[5,16,128]{2,1,0:T(8,128)S(1)} %get-tuple-element.18), channel_id=1, source_target_pairs={{0,8},{2,10},{4,12},{6,14},{8,16},{10,18},{12,20},{14,22},{16,24},... | collective-permute-start | bytes 122888 | tf_op jit(solution)/shard_map/ppermute | solution.py:303
  19.9 6.2 %collective-permute-start.5 = (f32[5,16,128]{2,1,0:T(8,128)S(1)}, f32[5,16,128]{2,1,0:T(8,128)S(1)}, u32[]{:S(2)}, u32[]{:S(2)}) collective-permute-start(f32[5,16,128]{2,1,0:T(8,128)S(1)} %get-tuple-element.19), channel_id=1, source_target_pairs={{0,16},{2,18},{4,20},{6,22},{8,24},{10,26},{12,28},{14,30},{16,0},... | collective-permute-start | bytes 122888 | tf_op jit(solution)/shard_map/ppermute | solution.py:303
  22.5 4.0 %collective-permute-start.6 = (f32[5,16,128]{2,1,0:T(8,128)S(1)}, f32[5,16,128]{2,1,0:T(8,128)S(1)}, u32[]{:S(2)}, u32[]{:S(2)}) collective-permute-start(f32[5,16,128]{2,1,0:T(8,128)S(1)} %get-tuple-element.20), channel_id=1, source_target_pairs={{0,24},{2,26},{4,28},{6,30},{8,0},{10,2},{12,4},{14,6},{16,8},{18,... | collective-permute-start | bytes 122888 | tf_op jit(solution)/shard_map/ppermute | solution.py:303

commit v9 on v8

--- a/solution.py
+++ b/solution.py
@@ -44,8 +44,8 @@
         piece = (slice(None), pl.ds(start, size))
         w_copies.append(pltpu.make_async_copy(w_hbm[i].at[piece], w_vmem[i].at[piece], w_sem.at[n]))
         x_copies.append(pltpu.make_async_copy(x_hbm[i].at[piece], x_vmem[i].at[piece], x_sem.at[n]))
+        x_copies[n].start()
         w_copies[n].start()
-        x_copies[n].start()
     tokens, rank = x_vmem[0].shape[0], w_vmem[0].shape[0]
     part = tokens // halves
     totals = {}
@@ -82,19 +82,21 @@
     )(*xs, *ws)
 
 
-def stage_kernel(low_ref, out_ref):
-    out_ref[...] = low_ref[...]
-
-
-def stage(low):
+def stage_kernel(low_ref, wanted_ref, low_out, wanted_out):
+    low_out[...] = low_ref[...]
+    wanted_out[...] = wanted_ref[...]
+
+
+def stage(low, wanted):
+    vmem = pl.BlockSpec(memory_space=pltpu.VMEM)
     return pl.pallas_call(
         stage_kernel,
-        out_shape=jax.ShapeDtypeStruct(low.shape, low.dtype),
-        in_specs=[pl.BlockSpec(memory_space=pltpu.VMEM)],
-        out_specs=pl.BlockSpec(memory_space=pltpu.VMEM),
+        out_shape=[jax.ShapeDtypeStruct(x.shape, x.dtype) for x in (low, wanted)],
+        in_specs=[vmem] * 2,
+        out_specs=[vmem] * 2,
         compiler_params=pltpu.CompilerParams(vmem_limit_bytes=SMALL_BYTES),
         name="stage",
-    )(low)
+    )(low, wanted)
 
 
 def vectors_kernel(n_parts, n_sends, *refs):
@@ -287,11 +289,12 @@
         (o_inputs, o_gradients, up_inputs, up_gradients),
         (o_in_proj.T, o_out_proj.T, up_in_proj.T, up_out_proj.T),
     )
+    wanted = jnp.broadcast_to((owner_map * own_rows // LANES)[:, None, None], (dp_count, EX_DEV, LANES))
     if tensor_count == 2:
-        parts = (stage(own), lax.ppermute(own, "tensor", [(0, 1), (1, 0)]))
+        staged, wanted = stage(own, wanted)
+        parts = (staged, lax.ppermute(own, "tensor", [(0, 1), (1, 0)]))
     else:
         parts = (lax.psum(own, "tensor"),)
-    wanted = jnp.broadcast_to((owner_map * own_rows // LANES)[:, None, None], (dp_count, EX_DEV, LANES))
     col_slabs = col_width // LANES
     if dp_count == len(FIRST) * len(SECOND) and own_rows == LANES:
         block = (2 * col_slabs + len(SECOND),)

time: 27.6 us -> 27.5 us (level)
  no operation moved by 1% of the time
where the time goes in v9:
time: 27.5 us; the launch traced here: 27.3 us
  starting transfers between devices  10.6 us (39%)
  waiting for transfers between devices  8.3 us (30%)
  Pallas kernels  7.68 us (28%)
  between operations  0.69 us (3%)
    pallas_call x1, Pallas kernels, project(): pl.pallas_call(functools.partial(project_kernel, plan, halves), out_shape...  6.33 us
    ppermute x3, starting transfers between devices, shards(): lax.ppermute(recv[n], 'dp', [(i, i + step & LAST) for i in range(dp_count)])  5.61 us
    ppermute x1, waiting for transfers between devices, shards(): parts = (staged, lax.ppermute(own, 'tensor', [(0, 1), (1, 0)]))  3.39 us
    ppermute x1, starting transfers between devices, shards(): parts = (staged, lax.ppermute(own, 'tensor', [(0, 1), (1, 0)]))  3.03 us
    ppermute x3, waiting for transfers between devices, shards(): lax.ppermute(recv[n], 'dp', [(i, i + step & LAST) for i in range(dp_count)])  2.67 us
    ppermute x3, waiting for transfers between devices, shards(): lax.ppermute(blocks[n], 'dp', [(i, i ^ step) for i in range(dp_count)])  2.24 us
    ppermute x3, starting transfers between devices, shards(): lax.ppermute(blocks[n], 'dp', [(i, i ^ step) for i in range(dp_count)])  1.93 us
    pallas_call x1, Pallas kernels, fisher(): pl.pallas_call(functools.partial(fisher_kernel, 1.0 / examples, len(parts...  0.94 us
  transfers between devices with their start and end apart: 7, of which 6 were waited for; matrix products, arithmetic and copies ran while one was open for 0% of the time, Pallas kernels for 0%

profile of v9, /device:TPU:0, one launch (start us, length us, event | category | flops | bytes accessed | tf_op | source)
XLA Modules:
  0.0 27.3 jit_solution(6956239473157323826)
XLA Ops:
  0.6 0.0 copy-start.1
  0.6 0.0 copy-start
  0.7 6.3 %project.1.low_ref = f32[2,128,128]{2,1,0:T(8,128)S(1)} custom-call(bf16[256,4096]{1,0:T(8,128)(2,1)} %refs_0_.1, bf16[256,4096]{1,0:T(8,128)(2,1)} %refs_1_.1, bf16[256,4096]{1,0:T(8,128)(2,1)} %refs_2_.2, bf16[256,14336]{1,0:T(8,128)(2,1)} %refs_3_.1, bf16[32,4096]{1,0:T(8,128)(2,1)} %bitcast.13, bf16[32,4096]{1,0:T(8,128)(2,1)} %bitcast.14, ...), custom_call_target="tpu_custom_call" | custom-call | tf_op jit(solution)/shard_map/project/pallas_call | solution.py:72
  7.0 3.0 %collective-permute-start = (f32[2,128,128]{2,1,0:T(8,128)S(1)}, f32[2,128,128]{2,1,0:T(8,128)S(1)}, u32[]{:S(2)}, u32[]{:S(2)}) collective-permute-start(f32[2,128,128]{2,1,0:T(8,128)S(1)} %project.1.low_ref), channel_id=1, source_target_pairs={{0,1},{1,0},{2,3},{3,2},{4,5},{5,4},{6,7},{7,6},{8,9},{9,8},{10,11... | collective-permute-start | bytes 393224 | tf_op jit(solution)/shard_map/ppermute | solution.py:295
  10.0 0.0 copy-done.1
  10.0 0.1 broadcast_in_dim.18.wanted_ref
  10.1 3.4 %collective-permute-done.refs_1_ = f32[2,128,128]{2,1,0:T(8,128)S(1)} collective-permute-done((f32[2,128,128]{2,1,0:T(8,128)S(1)}, f32[2,128,128]{2,1,0:T(8,128)S(1)}, u32[]{:S(2)}, u32[]{:S(2)}) %collective-permute-start) | collective-permute-done | bytes 131104 | tf_op jit(solution)/shard_map/ppermute | solution.py:295
  13.5 0.0 copy-done
  13.5 0.4 %vectors.1 = (f32[2,4,512]{2,1,0:T(4,128)S(1)}, f32[12,4,128]{2,1,0:T(4,128)S(1)}, f32[12,4,128]{2,1,0:T(4,128)S(1)}, f32[12,4,128]{2,1,0:T(4,128)S(1)}, f32[12,4,128]{2,1,0:T(4,128)S(1)}) custom-call(f32[2,128,128]{2,1,0:T(8,128)S(1)} %get-tuple-element.15.refs_0_, f32[2,128,128]{2,1,0:T(8,128)S(1)} %collective-permute-done.refs_1_, s32[1,256]{1,0:T(1,128)S(1)} %copy-done, ...), custom_call_target="tpu_custom_call" | custom-call | tf_op jit(solution)/shard_map/vectors/pallas_call | solution.py:167
  13.9 0.3 %collective-permute-start.1 = (f32[12,4,128]{2,1,0:T(4,128)S(1)}, f32[12,4,128]{2,1,0:T(4,128)S(1)}, u32[]{:S(2)}, u32[]{:S(2)}) collective-permute-start(f32[12,4,128]{2,1,0:T(4,128)S(1)} %get-tuple-element.18), channel_id=1, source_target_pairs={{0,6},{2,4},{4,2},{6,0},{8,14},{10,12},{12,10},{14,8},{16,22},{18,... | collective-permute-start | bytes 73736 | tf_op jit(solution)/shard_map/ppermute | solution.py:303
  14.2 1.5 %collective-permute-start.2 = (f32[12,4,128]{2,1,0:T(4,128)S(1)}, f32[12,4,128]{2,1,0:T(4,128)S(1)}, u32[]{:S(2)}, u32[]{:S(2)}) collective-permute-start(f32[12,4,128]{2,1,0:T(4,128)S(1)} %get-tuple-element.19), channel_id=1, source_target_pairs={{0,4},{2,6},{4,0},{6,2},{8,12},{10,14},{12,8},{14,10},{16,20},{18,... | collective-permute-start | bytes 73736 | tf_op jit(solution)/shard_map/ppermute | solution.py:303
  15.8 0.1 collective-permute-start.3
  15.8 1.4 %collective-permute-done.1.refs_1_ = f32[12,4,128]{2,1,0:T(4,128)S(1)} collective-permute-done((f32[12,4,128]{2,1,0:T(4,128)S(1)}, f32[12,4,128]{2,1,0:T(4,128)S(1)}, u32[]{:S(2)}, u32[]{:S(2)}) %collective-permute-start.1) | collective-permute-done | bytes 24608 | tf_op jit(solution)/shard_map/ppermute | solution.py:303
  17.2 0.8 %collective-permute-done.2.refs_2_ = f32[12,4,128]{2,1,0:T(4,128)S(1)} collective-permute-done((f32[12,4,128]{2,1,0:T(4,128)S(1)}, f32[12,4,128]{2,1,0:T(4,128)S(1)}, u32[]{:S(2)}, u32[]{:S(2)}) %collective-permute-start.2) | collective-permute-done | bytes 24608 | tf_op jit(solution)/shard_map/ppermute | solution.py:303
  18.1 0.0 collective-permute-done.3.refs_3_
  18.1 1.7 %collective-permute-start.4 = (f32[5,16,128]{2,1,0:T(8,128)S(1)}, f32[5,16,128]{2,1,0:T(8,128)S(1)}, u32[]{:S(2)}, u32[]{:S(2)}) collective-permute-start(f32[5,16,128]{2,1,0:T(8,128)S(1)} %get-tuple-element.22), channel_id=1, source_target_pairs={{0,8},{2,10},{4,12},{6,14},{8,16},{10,18},{12,20},{14,22},{16,24},... | collective-permute-start | bytes 122888 | tf_op jit(solution)/shard_map/ppermute | solution.py:306
  19.8 2.6 %collective-permute-start.5 = (f32[5,16,128]{2,1,0:T(8,128)S(1)}, f32[5,16,128]{2,1,0:T(8,128)S(1)}, u32[]{:S(2)}, u32[]{:S(2)}) collective-permute-start(f32[5,16,128]{2,1,0:T(8,128)S(1)} %get-tuple-element.23), channel_id=1, source_target_pairs={{0,16},{2,18},{4,20},{6,22},{8,24},{10,26},{12,28},{14,30},{16,0},... | collective-permute-start | bytes 122888 | tf_op jit(solution)/shard_map/ppermute | solution.py:306
  22.4 1.4 %collective-permute-start.6 = (f32[5,16,128]{2,1,0:T(8,128)S(1)}, f32[5,16,128]{2,1,0:T(8,128)S(1)}, u32[]{:S(2)}, u32[]{:S(2)}) collective-permute-start(f32[5,16,128]{2,1,0:T(8,128)S(1)} %get-tuple-element.24), channel_id=1, source_target_pairs={{0,24},{2,26},{4,28},{6,30},{8,0},{10,2},{12,4},{14,6},{16,8},{18,... | collective-permute-start | bytes 122888 | tf_op jit(solution)/shard_map/ppermute | solution.py:306
  23.7 0.3 collective-permute-done.4
  24.0 2.0 %collective-permute-done.5 = f32[5,16,128]{2,1,0:T(8,128)S(1)} collective-permute-done((f32[5,16,128]{2,1,0:T(8,128)S(1)}, f32[5,16,128]{2,1,0:T(8,128)S(1)}, u32[]{:S(2)}, u32[]{:S(2)}) %collective-permute-start.5) | collective-permute-done | bytes 40992 | tf_op jit(solution)/shard_map/ppermute | solution.py:306
  26.0 0.4 %collective-permute-done.6 = f32[5,16,128]{2,1,0:T(8,128)S(1)} collective-permute-done((f32[5,16,128]{2,1,0:T(8,128)S(1)}, f32[5,16,128]{2,1,0:T(8,128)S(1)}, u32[]{:S(2)}, u32[]{:S(2)}) %collective-permute-start.6) | collective-permute-done | bytes 40992 | tf_op jit(solution)/shard_map/ppermute | solution.py:306
  26.4 0.9 %fisher.1 = (f32[1,128,512]{2,1,0:T(8,128)}, f32[2,4,512]{2,1,0:T(4,128)}) custom-call(f32[1,5,16,128]{3,2,1,0:T(8,128)S(1)} %bitcast.8, f32[1,5,16,128]{3,2,1,0:T(8,128)S(1)} %bitcast.9, f32[1,5,16,128]{3,2,1,0:T(8,128)S(1)} %bitcast.10, f32[1,5,16,128]{3,2,1,0:T(8,128)S(1)} %bitcast.11, f32[2,4,512]{2,1,0:T(4,128)S(1)} %get-tuple-element.25.refs_4_), custom_call_target="tpu_custom_call" | custom-call | tf_op jit(solution)/shard_map/fisher/pallas_call | solution.py:252
  (3 shorter events, 0.1 us)
Async XLA Ops:
  0.6 9.4 %copy-start.1 = (s32[16]{0:T(128)S(1)}, s32[16]{0:T(128)}, u32[]{:S(2)}) copy-start(s32[16]{0:T(128)} %param.19) | copy-start | bytes 196
  0.6 12.9 %copy-start = (s32[1,256]{1,0:T(1,128)S(1)}, s32[1,256]{1,0:T(1,128)}, u32[]{:S(2)}) copy-start(s32[1,256]{1,0:T(1,128)} %refs_2_.3) | copy-start | bytes 3076
  7.0 6.5 %collective-permute-start = (f32[2,128,128]{2,1,0:T(8,128)S(1)}, f32[2,128,128]{2,1,0:T(8,128)S(1)}, u32[]{:S(2)}, u32[]{:S(2)}) collective-permute-start(f32[2,128,128]{2,1,0:T(8,128)S(1)} %project.1.low_ref), channel_id=1, source_target_pairs={{0,1},{1,0},{2,3},{3,2},{4,5},{5,4},{6,7},{7,6},{8,9},{9,8},{10,11... | collective-permute-start | bytes 393224 | tf_op jit(solution)/shard_map/ppermute | solution.py:295
  13.9 3.3 %collective-permute-start.1 = (f32[12,4,128]{2,1,0:T(4,128)S(1)}, f32[12,4,128]{2,1,0:T(4,128)S(1)}, u32[]{:S(2)}, u32[]{:S(2)}) collective-permute-start(f32[12,4,128]{2,1,0:T(4,128)S(1)} %get-tuple-element.18), channel_id=1, source_target_pairs={{0,6},{2,4},{4,2},{6,0},{8,14},{10,12},{12,10},{14,8},{16,22},{18,... | collective-permute-start | bytes 73736 | tf_op jit(solution)/shard_map/ppermute | solution.py:303
  14.2 3.8 %collective-permute-start.2 = (f32[12,4,128]{2,1,0:T(4,128)S(1)}, f32[12,4,128]{2,1,0:T(4,128)S(1)}, u32[]{:S(2)}, u32[]{:S(2)}) collective-permute-start(f32[12,4,128]{2,1,0:T(4,128)S(1)} %get-tuple-element.19), channel_id=1, source_target_pairs={{0,4},{2,6},{4,0},{6,2},{8,12},{10,14},{12,8},{14,10},{16,20},{18,... | collective-permute-start | bytes 73736 | tf_op jit(solution)/shard_map/ppermute | solution.py:303
  15.8 2.3 %collective-permute-start.3 = (f32[12,4,128]{2,1,0:T(4,128)S(1)}, f32[12,4,128]{2,1,0:T(4,128)S(1)}, u32[]{:S(2)}, u32[]{:S(2)}) collective-permute-start(f32[12,4,128]{2,1,0:T(4,128)S(1)} %get-tuple-element.20), channel_id=1, source_target_pairs={{0,2},{2,0},{4,6},{6,4},{8,10},{10,8},{12,14},{14,12},{16,18},{18,... | collective-permute-start | bytes 73736 | tf_op jit(solution)/shard_map/ppermute | solution.py:303
  18.1 5.9 %collective-permute-start.4 = (f32[5,16,128]{2,1,0:T(8,128)S(1)}, f32[5,16,128]{2,1,0:T(8,128)S(1)}, u32[]{:S(2)}, u32[]{:S(2)}) collective-permute-start(f32[5,16,128]{2,1,0:T(8,128)S(1)} %get-tuple-element.22), channel_id=1, source_target_pairs={{0,8},{2,10},{4,12},{6,14},{8,16},{10,18},{12,20},{14,22},{16,24},... | collective-permute-start | bytes 122888 | tf_op jit(solution)/shard_map/ppermute | solution.py:306
  19.8 6.2 %collective-permute-start.5 = (f32[5,16,128]{2,1,0:T(8,128)S(1)}, f32[5,16,128]{2,1,0:T(8,128)S(1)}, u32[]{:S(2)}, u32[]{:S(2)}) collective-permute-start(f32[5,16,128]{2,1,0:T(8,128)S(1)} %get-tuple-element.23), channel_id=1, source_target_pairs={{0,16},{2,18},{4,20},{6,22},{8,24},{10,26},{12,28},{14,30},{16,0},... | collective-permute-start | bytes 122888 | tf_op jit(solution)/shard_map/ppermute | solution.py:306
  22.4 4.0 %collective-permute-start.6 = (f32[5,16,128]{2,1,0:T(8,128)S(1)}, f32[5,16,128]{2,1,0:T(8,128)S(1)}, u32[]{:S(2)}, u32[]{:S(2)}) collective-permute-start(f32[5,16,128]{2,1,0:T(8,128)S(1)} %get-tuple-element.24), channel_id=1, source_target_pairs={{0,24},{2,26},{4,28},{6,30},{8,0},{10,2},{12,4},{14,6},{16,8},{18,... | collective-permute-start | bytes 122888 | tf_op jit(solution)/shard_map/ppermute | solution.py:306

commit v10 on v9

--- a/solution.py
+++ b/solution.py
@@ -209,13 +209,13 @@
 def fisher_kernel(scale, n_parts, *refs):
     parts, vec_ref, (out_ref, vec_out, stack, full, sems) = refs[:n_parts], refs[n_parts], refs[-5:]
     store = pltpu.make_async_copy(vec_ref, vec_out, sems.at[0])
-    store.start()
     examples, slabs = stack.shape[0], stack.shape[1] // LANES
     pieces = [part.at[i] for part in parts for i in range(part.shape[0])]
     rows = examples // len(pieces)
     for i, piece in enumerate(pieces):
         for k in range(slabs):
             stack[pl.ds(i * rows, rows), pl.ds(k * LANES, LANES)] = piece[k]
+    store.start()
     own_rows, col_width = out_ref.shape[1:]
     start = 0
     if own_rows < LANES:

time: 27.5 us -> 27.5 us (level)
  no operation moved by 1% of the time
where the time goes in v10:
time: 27.5 us; the launch traced here: 27.3 us
  starting transfers between devices  10.6 us (39%)
  waiting for transfers between devices  8.3 us (30%)
  Pallas kernels  7.68 us (28%)
  between operations  0.69 us (3%)
    pallas_call x1, Pallas kernels, project(): pl.pallas_call(functools.partial(project_kernel, plan, halves), out_shape...  6.33 us
    ppermute x3, starting transfers between devices, shards(): lax.ppermute(recv[n], 'dp', [(i, i + step & LAST) for i in range(dp_count)])  5.61 us
    ppermute x1, waiting for transfers between devices, shards(): parts = (staged, lax.ppermute(own, 'tensor', [(0, 1), (1, 0)]))  3.39 us
    ppermute x1, starting transfers between devices, shards(): parts = (staged, lax.ppermute(own, 'tensor', [(0, 1), (1, 0)]))  3.03 us
    ppermute x3, waiting for transfers between devices, shards(): lax.ppermute(recv[n], 'dp', [(i, i + step & LAST) for i in range(dp_count)])  2.67 us
    ppermute x3, waiting for transfers between devices, shards(): lax.ppermute(blocks[n], 'dp', [(i, i ^ step) for i in range(dp_count)])  2.24 us
    ppermute x3, starting transfers between devices, shards(): lax.ppermute(blocks[n], 'dp', [(i, i ^ step) for i in range(dp_count)])  1.93 us
    pallas_call x1, Pallas kernels, fisher(): pl.pallas_call(functools.partial(fisher_kernel, 1.0 / examples, len(parts...  0.94 us
  transfers between devices with their start and end apart: 7, of which 6 were waited for; matrix products, arithmetic and copies ran while one was open for 0% of the time, Pallas kernels for 0%

profile of v10, /device:TPU:0, one launch (start us, length us, event | category | flops | bytes accessed | tf_op | source)
XLA Modules:
  0.0 27.3 jit_solution(6956239473157323826)
XLA Ops:
  0.6 0.0 copy-start.1
  0.6 0.0 copy-start
  0.7 6.3 %project.1.low_ref = f32[2,128,128]{2,1,0:T(8,128)S(1)} custom-call(bf16[256,4096]{1,0:T(8,128)(2,1)} %refs_0_.1, bf16[256,4096]{1,0:T(8,128)(2,1)} %refs_1_.1, bf16[256,4096]{1,0:T(8,128)(2,1)} %refs_2_.2, bf16[256,14336]{1,0:T(8,128)(2,1)} %refs_3_.1, bf16[32,4096]{1,0:T(8,128)(2,1)} %bitcast.13, bf16[32,4096]{1,0:T(8,128)(2,1)} %bitcast.14, ...), custom_call_target="tpu_custom_call" | custom-call | tf_op jit(solution)/shard_map/project/pallas_call | solution.py:72
  7.0 3.0 %collective-permute-start = (f32[2,128,128]{2,1,0:T(8,128)S(1)}, f32[2,128,128]{2,1,0:T(8,128)S(1)}, u32[]{:S(2)}, u32[]{:S(2)}) collective-permute-start(f32[2,128,128]{2,1,0:T(8,128)S(1)} %project.1.low_ref), channel_id=1, source_target_pairs={{0,1},{1,0},{2,3},{3,2},{4,5},{5,4},{6,7},{7,6},{8,9},{9,8},{10,11... | collective-permute-start | bytes 393224 | tf_op jit(solution)/shard_map/ppermute | solution.py:295
  10.0 0.0 copy-done.1
  10.0 0.1 broadcast_in_dim.18.wanted_ref
  10.1 3.4 %collective-permute-done.refs_1_ = f32[2,128,128]{2,1,0:T(8,128)S(1)} collective-permute-done((f32[2,128,128]{2,1,0:T(8,128)S(1)}, f32[2,128,128]{2,1,0:T(8,128)S(1)}, u32[]{:S(2)}, u32[]{:S(2)}) %collective-permute-start) | collective-permute-done | bytes 131104 | tf_op jit(solution)/shard_map/ppermute | solution.py:295
  13.5 0.0 copy-done
  13.5 0.4 %vectors.1 = (f32[2,4,512]{2,1,0:T(4,128)S(1)}, f32[12,4,128]{2,1,0:T(4,128)S(1)}, f32[12,4,128]{2,1,0:T(4,128)S(1)}, f32[12,4,128]{2,1,0:T(4,128)S(1)}, f32[12,4,128]{2,1,0:T(4,128)S(1)}) custom-call(f32[2,128,128]{2,1,0:T(8,128)S(1)} %get-tuple-element.15.refs_0_, f32[2,128,128]{2,1,0:T(8,128)S(1)} %collective-permute-done.refs_1_, s32[1,256]{1,0:T(1,128)S(1)} %copy-done, ...), custom_call_target="tpu_custom_call" | custom-call | tf_op jit(solution)/shard_map/vectors/pallas_call | solution.py:167
  13.9 0.3 %collective-permute-start.1 = (f32[12,4,128]{2,1,0:T(4,128)S(1)}, f32[12,4,128]{2,1,0:T(4,128)S(1)}, u32[]{:S(2)}, u32[]{:S(2)}) collective-permute-start(f32[12,4,128]{2,1,0:T(4,128)S(1)} %get-tuple-element.18), channel_id=1, source_target_pairs={{0,6},{2,4},{4,2},{6,0},{8,14},{10,12},{12,10},{14,8},{16,22},{18,... | collective-permute-start | bytes 73736 | tf_op jit(solution)/shard_map/ppermute | solution.py:303
  14.2 1.5 %collective-permute-start.2 = (f32[12,4,128]{2,1,0:T(4,128)S(1)}, f32[12,4,128]{2,1,0:T(4,128)S(1)}, u32[]{:S(2)}, u32[]{:S(2)}) collective-permute-start(f32[12,4,128]{2,1,0:T(4,128)S(1)} %get-tuple-element.19), channel_id=1, source_target_pairs={{0,4},{2,6},{4,0},{6,2},{8,12},{10,14},{12,8},{14,10},{16,20},{18,... | collective-permute-start | bytes 73736 | tf_op jit(solution)/shard_map/ppermute | solution.py:303
  15.8 0.1 collective-permute-start.3
  15.8 1.4 %collective-permute-done.1.refs_1_ = f32[12,4,128]{2,1,0:T(4,128)S(1)} collective-permute-done((f32[12,4,128]{2,1,0:T(4,128)S(1)}, f32[12,4,128]{2,1,0:T(4,128)S(1)}, u32[]{:S(2)}, u32[]{:S(2)}) %collective-permute-start.1) | collective-permute-done | bytes 24608 | tf_op jit(solution)/shard_map/ppermute | solution.py:303
  17.2 0.8 %collective-permute-done.2.refs_2_ = f32[12,4,128]{2,1,0:T(4,128)S(1)} collective-permute-done((f32[12,4,128]{2,1,0:T(4,128)S(1)}, f32[12,4,128]{2,1,0:T(4,128)S(1)}, u32[]{:S(2)}, u32[]{:S(2)}) %collective-permute-start.2) | collective-permute-done | bytes 24608 | tf_op jit(solution)/shard_map/ppermute | solution.py:303
  18.1 0.0 collective-permute-done.3.refs_3_
  18.1 1.7 %collective-permute-start.4 = (f32[5,16,128]{2,1,0:T(8,128)S(1)}, f32[5,16,128]{2,1,0:T(8,128)S(1)}, u32[]{:S(2)}, u32[]{:S(2)}) collective-permute-start(f32[5,16,128]{2,1,0:T(8,128)S(1)} %get-tuple-element.22), channel_id=1, source_target_pairs={{0,8},{2,10},{4,12},{6,14},{8,16},{10,18},{12,20},{14,22},{16,24},... | collective-permute-start | bytes 122888 | tf_op jit(solution)/shard_map/ppermute | solution.py:306
  19.8 2.6 %collective-permute-start.5 = (f32[5,16,128]{2,1,0:T(8,128)S(1)}, f32[5,16,128]{2,1,0:T(8,128)S(1)}, u32[]{:S(2)}, u32[]{:S(2)}) collective-permute-start(f32[5,16,128]{2,1,0:T(8,128)S(1)} %get-tuple-element.23), channel_id=1, source_target_pairs={{0,16},{2,18},{4,20},{6,22},{8,24},{10,26},{12,28},{14,30},{16,0},... | collective-permute-start | bytes 122888 | tf_op jit(solution)/shard_map/ppermute | solution.py:306
  22.4 1.4 %collective-permute-start.6 = (f32[5,16,128]{2,1,0:T(8,128)S(1)}, f32[5,16,128]{2,1,0:T(8,128)S(1)}, u32[]{:S(2)}, u32[]{:S(2)}) collective-permute-start(f32[5,16,128]{2,1,0:T(8,128)S(1)} %get-tuple-element.24), channel_id=1, source_target_pairs={{0,24},{2,26},{4,28},{6,30},{8,0},{10,2},{12,4},{14,6},{16,8},{18,... | collective-permute-start | bytes 122888 | tf_op jit(solution)/shard_map/ppermute | solution.py:306
  23.7 0.3 collective-permute-done.4
  24.0 2.0 %collective-permute-done.5 = f32[5,16,128]{2,1,0:T(8,128)S(1)} collective-permute-done((f32[5,16,128]{2,1,0:T(8,128)S(1)}, f32[5,16,128]{2,1,0:T(8,128)S(1)}, u32[]{:S(2)}, u32[]{:S(2)}) %collective-permute-start.5) | collective-permute-done | bytes 40992 | tf_op jit(solution)/shard_map/ppermute | solution.py:306
  26.0 0.4 %collective-permute-done.6 = f32[5,16,128]{2,1,0:T(8,128)S(1)} collective-permute-done((f32[5,16,128]{2,1,0:T(8,128)S(1)}, f32[5,16,128]{2,1,0:T(8,128)S(1)}, u32[]{:S(2)}, u32[]{:S(2)}) %collective-permute-start.6) | collective-permute-done | bytes 40992 | tf_op jit(solution)/shard_map/ppermute | solution.py:306
  26.4 0.9 %fisher.1 = (f32[1,128,512]{2,1,0:T(8,128)}, f32[2,4,512]{2,1,0:T(4,128)}) custom-call(f32[1,5,16,128]{3,2,1,0:T(8,128)S(1)} %bitcast.8, f32[1,5,16,128]{3,2,1,0:T(8,128)S(1)} %bitcast.9, f32[1,5,16,128]{3,2,1,0:T(8,128)S(1)} %bitcast.10, f32[1,5,16,128]{3,2,1,0:T(8,128)S(1)} %bitcast.11, f32[2,4,512]{2,1,0:T(4,128)S(1)} %get-tuple-element.25.refs_4_), custom_call_target="tpu_custom_call" | custom-call | tf_op jit(solution)/shard_map/fisher/pallas_call | solution.py:252
  (3 shorter events, 0.1 us)
Async XLA Ops:
  0.6 9.4 %copy-start.1 = (s32[16]{0:T(128)S(1)}, s32[16]{0:T(128)}, u32[]{:S(2)}) copy-start(s32[16]{0:T(128)} %param.19) | copy-start | bytes 196
  0.6 12.9 %copy-start = (s32[1,256]{1,0:T(1,128)S(1)}, s32[1,256]{1,0:T(1,128)}, u32[]{:S(2)}) copy-start(s32[1,256]{1,0:T(1,128)} %refs_2_.3) | copy-start | bytes 3076
  7.0 6.5 %collective-permute-start = (f32[2,128,128]{2,1,0:T(8,128)S(1)}, f32[2,128,128]{2,1,0:T(8,128)S(1)}, u32[]{:S(2)}, u32[]{:S(2)}) collective-permute-start(f32[2,128,128]{2,1,0:T(8,128)S(1)} %project.1.low_ref), channel_id=1, source_target_pairs={{0,1},{1,0},{2,3},{3,2},{4,5},{5,4},{6,7},{7,6},{8,9},{9,8},{10,11... | collective-permute-start | bytes 393224 | tf_op jit(solution)/shard_map/ppermute | solution.py:295
  13.9 3.3 %collective-permute-start.1 = (f32[12,4,128]{2,1,0:T(4,128)S(1)}, f32[12,4,128]{2,1,0:T(4,128)S(1)}, u32[]{:S(2)}, u32[]{:S(2)}) collective-permute-start(f32[12,4,128]{2,1,0:T(4,128)S(1)} %get-tuple-element.18), channel_id=1, source_target_pairs={{0,6},{2,4},{4,2},{6,0},{8,14},{10,12},{12,10},{14,8},{16,22},{18,... | collective-permute-start | bytes 73736 | tf_op jit(solution)/shard_map/ppermute | solution.py:303
  14.2 3.8 %collective-permute-start.2 = (f32[12,4,128]{2,1,0:T(4,128)S(1)}, f32[12,4,128]{2,1,0:T(4,128)S(1)}, u32[]{:S(2)}, u32[]{:S(2)}) collective-permute-start(f32[12,4,128]{2,1,0:T(4,128)S(1)} %get-tuple-element.19), channel_id=1, source_target_pairs={{0,4},{2,6},{4,0},{6,2},{8,12},{10,14},{12,8},{14,10},{16,20},{18,... | collective-permute-start | bytes 73736 | tf_op jit(solution)/shard_map/ppermute | solution.py:303
  15.8 2.3 %collective-permute-start.3 = (f32[12,4,128]{2,1,0:T(4,128)S(1)}, f32[12,4,128]{2,1,0:T(4,128)S(1)}, u32[]{:S(2)}, u32[]{:S(2)}) collective-permute-start(f32[12,4,128]{2,1,0:T(4,128)S(1)} %get-tuple-element.20), channel_id=1, source_target_pairs={{0,2},{2,0},{4,6},{6,4},{8,10},{10,8},{12,14},{14,12},{16,18},{18,... | collective-permute-start | bytes 73736 | tf_op jit(solution)/shard_map/ppermute | solution.py:303
  18.1 5.9 %collective-permute-start.4 = (f32[5,16,128]{2,1,0:T(8,128)S(1)}, f32[5,16,128]{2,1,0:T(8,128)S(1)}, u32[]{:S(2)}, u32[]{:S(2)}) collective-permute-start(f32[5,16,128]{2,1,0:T(8,128)S(1)} %get-tuple-element.22), channel_id=1, source_target_pairs={{0,8},{2,10},{4,12},{6,14},{8,16},{10,18},{12,20},{14,22},{16,24},... | collective-permute-start | bytes 122888 | tf_op jit(solution)/shard_map/ppermute | solution.py:306
  19.8 6.2 %collective-permute-start.5 = (f32[5,16,128]{2,1,0:T(8,128)S(1)}, f32[5,16,128]{2,1,0:T(8,128)S(1)}, u32[]{:S(2)}, u32[]{:S(2)}) collective-permute-start(f32[5,16,128]{2,1,0:T(8,128)S(1)} %get-tuple-element.23), channel_id=1, source_target_pairs={{0,16},{2,18},{4,20},{6,22},{8,24},{10,26},{12,28},{14,30},{16,0},... | collective-permute-start | bytes 122888 | tf_op jit(solution)/shard_map/ppermute | solution.py:306
  22.4 4.0 %collective-permute-start.6 = (f32[5,16,128]{2,1,0:T(8,128)S(1)}, f32[5,16,128]{2,1,0:T(8,128)S(1)}, u32[]{:S(2)}, u32[]{:S(2)}) collective-permute-start(f32[5,16,128]{2,1,0:T(8,128)S(1)} %get-tuple-element.24), channel_id=1, source_target_pairs={{0,24},{2,26},{4,28},{6,30},{8,0},{10,2},{12,4},{14,6},{16,8},{18,... | collective-permute-start | bytes 122888 | tf_op jit(solution)/shard_map/ppermute | solution.py:306
